TPU v7x, 256 devices: a whole 4x4x8 slice. The times are simulated.
256 devices in a mesh: bead: 8 (over x, core), space: 32 (over z, y).
Axes of the slice: x: 4, y: 4, z: 8, core: 2. Of those that a mesh axis runs over, the one named last changes fastest.
Arguments:
- charges: float32 [32, 512, 128, 128], P('bead', 'space'), parts along dimension 0, may hold values from -6 to 6
- kernel_taps: float32 [4, 4, 3, 15], replicated, may hold values from -1.5 to 1.5
Outputs:
- potential: float32 [32, 512, 128, 128], P('bead', 'space'), parts along dimension 0
There are 8 independent parts, one for each index of `bead`. A program takes and returns all parts, laid end to end along the dimension named above; an argument that names none is the same for every part. Nothing has to cross between parts.
All inputs are finite; a program needn't handle non-finite values.
Results may differ from a plain program's by a relative error of at most 0.0001.
Values sent between devices are 32-bit elements; how exact they have to be, the bound alone decides.
No kernel may reach another device: no remote copies, remote signals or barrier semaphores. Data moves between devices by JAX's collectives and lax.ppermute only.
A program may use at most 128 MiB of HBM per device.

v0:
```python
import functools

import jax
import jax.numpy as jnp
import ml_dtypes
import numpy as np
from jax import lax
from jax.experimental import pallas as pl
from jax.experimental.pallas import tpu as pltpu
from jax.sharding import PartitionSpec as P

REACH = 7
TAPS = 15
SIDE = 128
SLAB = 16
COUNT = 32
F32 = jnp.float32
BF16 = jnp.bfloat16
CUBIC = {0: 1.0, 1: 0.5625, -1: 0.5625, 3: -0.0625, -3: -0.0625}


def symbol(side):
    theta = 2.0 * np.pi * np.arange(side) / side
    return 1.0 + 1.125 * np.cos(theta) - 0.125 * np.cos(3.0 * theta)


def split_const(matrix):
    high = matrix.astype(ml_dtypes.bfloat16)
    low = (matrix - high.astype(np.float64)).astype(ml_dtypes.bfloat16)
    return high, low


def dft_parts():
    angle = 2.0 * np.pi * (np.outer(np.arange(SIDE), np.arange(SIDE)) % SIDE) / SIDE
    c, s = np.cos(angle), np.sin(angle)
    fwd_x = np.block([[c, -s], [s, c]])
    fwd_y = np.block([[c, s], [-s, c]])
    inv_y = np.block([[c, -s], [s, c]]) / SIDE
    inv_x = np.block([[c, s], [-s, c]]) / SIDE
    return np.stack([part for m in (fwd_x, fwd_y, inv_y, inv_x) for part in split_const(m)])


def coarse_parts():
    restrict = np.zeros((64, SIDE))
    for j in range(64):
        for d, weight in CUBIC.items():
            restrict[j, (2 * j + d) % SIDE] += 0.5 * weight
    angle = 2.0 * np.pi * (np.outer(np.arange(64), np.arange(64)) % 64) / 64
    real, imag = np.cos(angle) @ restrict, -np.sin(angle) @ restrict
    along_x = np.block([[real.T, imag.T], [-imag.T, real.T]])
    along_y = np.block([[real, -imag], [imag, real]])
    xh, xl = split_const(along_x)
    yh, yl = split_const(along_y)
    return np.concatenate([np.concatenate([xh, xl], 1), yh, yl], 0)


def fold_weights():
    half = np.outer(symbol(64), symbol(64)) / 16.0
    quarter = np.outer(symbol(32), symbol(32)) / 16.0
    half = np.tile(half, (1, 2))
    quarter = np.concatenate([quarter, quarter * 0, quarter, quarter * 0], axis=1)
    return np.concatenate([half, quarter], 0).astype(np.float32)


def spread_weights():
    full = np.outer(symbol(128), symbol(128))
    half = np.tile(np.outer(symbol(64), symbol(64)), (1, 2))
    return full.astype(np.float32), half.astype(np.float32)


def split(value):
    high = value.astype(BF16)
    return high, (value - high.astype(F32)).astype(BF16)


def dot(a, b):
    return jnp.dot(a, b, preferred_element_type=F32)


def right_mul(value, high, low):
    vh, vl = split(value)
    return dot(vh, high) + dot(vl, high) + dot(vh, low)


def left_mul(high, low, value):
    vh, vl = split(value)
    return dot(high, vh) + dot(high, vl) + dot(low, vh)


def params(megabytes=16):
    return pltpu.CompilerParams(vmem_limit_bytes=megabytes * 1024 * 1024)


def whole(shape):
    return pl.BlockSpec(shape, lambda *_: (0,) * len(shape))


def forward_layer(v, mats, out):
    rows = jnp.concatenate(
        [jnp.concatenate([v[0, 0], v[1, 0]], 1), jnp.concatenate([v[2, 0], v[3, 0]], 1)], 0
    )
    a = right_mul(rows, mats[0], mats[1])
    b = jnp.concatenate(
        [
            jnp.concatenate([a[:SIDE, :SIDE], a[:SIDE, SIDE:]], 0),
            jnp.concatenate([a[SIDE:, :SIDE], a[SIDE:, SIDE:]], 0),
        ],
        1,
    )
    c = left_mul(mats[2], mats[3], b)
    out[0, 0, 0] = c[:SIDE, :SIDE]
    out[0, 0, 1] = c[SIDE:, :SIDE]
    out[0, 1, 0] = c[:SIDE, SIDE:]
    out[0, 1, 1] = c[SIDE:, SIDE:]


def near_kernel(v_low, v_high, mats, own, from_below, from_above, token, out_low, out_high):
    step = pl.program_id(0)

    @pl.when(step < 3)
    def _():
        forward_layer(v_low, mats, out_low)
        forward_layer(v_high, mats, out_high)

    cells = [own[0] + from_below[0], own[1] + from_below[1]] + [own[c] for c in range(2, 7)]
    cells += [own[7] + from_above[0], own[8] + from_above[1]]
    for half in range(2):
        @pl.when(step == 3 + half)
        def _():
            for c in range(4):
                out_high[0, c // 2, c % 2] = cells[4 * half + c]
                out_low[0, c // 2, c % 2] = cells[4 * half + c + 1]


def near_layers(charges, mats, own, from_below, from_above, token):
    shape = jax.ShapeDtypeStruct((5, 2, 2, SIDE, SIDE), F32)
    block = pl.BlockSpec((1, 2, 2, SIDE, SIDE), lambda i: (i, 0, 0, 0, 0))
    return pl.pallas_call(
        near_kernel,
        grid=(5,),
        in_specs=[
            pl.BlockSpec((4, 1, SIDE, SIDE), lambda i: (0, jnp.minimum(i, 2), 0, 0)),
            pl.BlockSpec((4, 1, SIDE, SIDE), lambda i: (0, 13 + jnp.minimum(i, 2), 0, 0)),
            pl.BlockSpec((4, 256, 256), lambda i: (0, 0, 0)),
            whole((9, SIDE, SIDE)),
            whole((2, SIDE, SIDE)),
            whole((2, SIDE, SIDE)),
            pl.BlockSpec(memory_space=pl.ANY),
        ],
        out_specs=[block, block],
        out_shape=[shape, shape],
        compiler_params=params(),
        name="near",
        cost_estimate=pl.CostEstimate(flops=1200000000, bytes_accessed=5000000, transcendentals=0),
    )(charges, charges, mats, own, from_below, from_above, token)


def far_kernel(v_low, v_high, mats, token, out_low, out_high, mid_low, mid_high):
    step = pl.program_id(0)

    @pl.when(step < 4)
    def _():
        forward_layer(v_low, mats, out_low)
        forward_layer(v_high, mats, out_high)

    @pl.when(step == 4)
    def _():
        forward_layer(v_low, mats, mid_low)
        forward_layer(v_high, mats, mid_high)


def far_layers(charges, mats, token):
    shape = jax.ShapeDtypeStruct((4, 2, 2, SIDE, SIDE), F32)
    single = jax.ShapeDtypeStruct((1, 2, 2, SIDE, SIDE), F32)
    block = pl.BlockSpec((1, 2, 2, SIDE, SIDE), lambda i: (jnp.minimum(i, 3), 0, 0, 0, 0))
    fixed = pl.BlockSpec((1, 2, 2, SIDE, SIDE), lambda i: (0, 0, 0, 0, 0))
    return pl.pallas_call(
        far_kernel,
        grid=(5,),
        in_specs=[
            pl.BlockSpec((4, 1, SIDE, SIDE), lambda i: (0, 3 + i, 0, 0)),
            pl.BlockSpec((4, 1, SIDE, SIDE), lambda i: (0, jnp.where(i < 4, 9 + i, 8), 0, 0)),
            pl.BlockSpec((4, 256, 256), lambda i: (0, 0, 0)),
            pl.BlockSpec(memory_space=pl.ANY),
        ],
        out_specs=[block, block, fixed, fixed],
        out_shape=[shape, shape, single, single],
        compiler_params=params(),
        name="far",
        cost_estimate=pl.CostEstimate(flops=2000000000, bytes_accessed=6000000, transcendentals=0),
    )(charges, charges, mats, token)


def fold_lanes(value, lanes):
    return value + pltpu.roll(value, SIDE - lanes, 1)


def restrict_layers(layers, first, low, high):
    out = []
    for cell in range(low, high):
        total = None
        for d, weight in CUBIC.items():
            z = 2 * cell + d - first
            if 0 <= z < len(layers):
                term = (0.5 * weight) * layers[z]
                total = term if total is None else total + term
        out.append(total)
    return out


def partial_kernel(v_hbm, mats, weights, up_ref, down_ref, own_ref, pay_ref, v_ref, mid_ref, sems):
    def copy(k):
        layers = pl.ds(2 * k, 2)
        return pltpu.make_async_copy(v_hbm.at[:, layers], v_ref.at[:, layers], sems.at[k])

    for k in range(SLAB // 2):
        copy(k).start()
    arrived = 0
    lane = lax.broadcasted_iota(jnp.int32, (SIDE, SIDE), 1)
    half, quarter = weights[:64], weights[64:]
    for c in range(-1, 10):
        while arrived < min(SLAB // 2, (2 * c + 3) // 2 + 1):
            copy(arrived).wait()
            arrived += 1
        beads = []
        for bead in range(4):
            total = None
            for d, weight in CUBIC.items():
                z = 2 * c + d
                if 0 <= z < SLAB:
                    term = (0.5 * weight) * v_ref[bead, z]
                    total = term if total is None else total + term
            beads.append(total)
        rows = jnp.concatenate([jnp.concatenate(beads[:2], 1), jnp.concatenate(beads[2:], 1)], 0)
        a = right_mul(rows, mats[:256, :SIDE], mats[:256, SIDE:])
        first, second = a[:SIDE], a[SIDE:]
        real = jnp.where(lane < 64, first, pltpu.roll(second, 64, 1))
        imag = jnp.where(lane < 64, pltpu.roll(first, 64, 1), second)
        value = left_mul(mats[256:384], mats[384:], jnp.concatenate([real, imag], 0))
        mid_ref[c + 1] = value
        if 0 <= c <= 8:
            own_ref[c] = value
        if c in (8, 9):
            up_ref[c - 8] = value
        if c in (-1, 0):
            down_ref[c + 1] = value

    small = []
    for c in range(11):
        parts = []
        for part in range(2):
            g = half * mid_ref[c, 64 * part : 64 * part + 64]
            parts.append(fold_lanes(g[:32] + g[32:], 32))
        small.append(jnp.concatenate(parts, 0))
    level2 = restrict_layers(small, -1, -2, 7)
    lane = lax.broadcasted_iota(jnp.int32, (32, SIDE), 1)
    for c, value in enumerate(level2):
        packed = jnp.where((lane // 32) % 2 == 0, value[:32], pltpu.roll(value[32:], 32, 1))
        pay_ref[:, c, :] = packed

    tiny = []
    for value in level2:
        parts = []
        for part in range(2):
            g = quarter * value[32 * part : 32 * part + 32]
            parts.append(fold_lanes(g[:16] + g[16:], 16))
        tiny.append(jnp.concatenate(parts, 0))
    level3 = restrict_layers(tiny, -2, -2, 5)
    lane = lax.broadcasted_iota(jnp.int32, (16, SIDE), 1)
    for c, value in enumerate(level3):
        packed = jnp.where((lane // 16) % 2 == 0, value[:16], pltpu.roll(value[16:], 16, 1))
        pay_ref[:, 9 + c, :] = jnp.concatenate([packed, packed], 0)


def partial_sums(charges):
    outs = [(2, SIDE, SIDE), (2, SIDE, SIDE), (9, SIDE, SIDE), (COUNT, 16, SIDE)]
    return pl.pallas_call(
        partial_kernel,
        out_shape=[jax.ShapeDtypeStruct(s, F32) for s in outs],
        in_specs=[
            pl.BlockSpec(memory_space=pltpu.HBM),
            pl.BlockSpec(memory_space=pltpu.VMEM),
            pl.BlockSpec(memory_space=pltpu.VMEM),
        ],
        scratch_shapes=[
            pltpu.VMEM((4, SLAB, SIDE, SIDE), F32),
            pltpu.VMEM((11, SIDE, SIDE), F32),
            pltpu.SemaphoreType.DMA((SLAB // 2,)),
        ],
        compiler_params=params(),
        name="partial",
        cost_estimate=pl.CostEstimate(flops=500000000, bytes_accessed=6000000, transcendentals=0),
    )(charges, jnp.asarray(coarse_parts()), jnp.asarray(fold_weights()))


def gather_matrix():
    def places(rows, period, shift, low, high):
        r = lax.broadcasted_iota(jnp.int32, (rows, COUNT * 16), 0)
        q = lax.broadcasted_iota(jnp.int32, (rows, COUNT * 16), 1)
        c = q % 16
        z = (period // COUNT) * (q // 16) + c - low - 2
        hit = ((r - REACH - z) % period == 0) & (c >= low) & (c < high) & (r < period + 2 * REACH)
        return jnp.where(hit, 1.0, 0.0)

    return jnp.concatenate([places(144, 128, 0, 0, 9), places(80, 64, 0, 9, 16)], 0).astype(BF16)


def scatter_matrix():
    r = lax.broadcasted_iota(jnp.int32, (COUNT * 16, 256), 0)
    q = lax.broadcasted_iota(jnp.int32, (COUNT * 16, 256), 1)
    z = 4 * (r // 16) + r % 16 - 2
    same = (z - q) % 128 == 0
    d = jnp.abs((z - 2 * (q - 128) + 64) % 128 - 64)
    weight = jnp.where(d == 0, 1.0, jnp.where(d == 1, 0.5625, jnp.where(d == 3, -0.0625, 0.0)))
    value = jnp.where(q < 128, jnp.where(same, 1.0, 0.0), jnp.where(q < 192, weight, 0.0))
    return jnp.where(r % 16 < 9, value, 0.0).astype(BF16)


def swap_lanes(value, lanes):
    lane = lax.broadcasted_iota(jnp.int32, value.shape, 1)
    return jnp.where((lane // lanes) % 2 == 0, pltpu.roll(value, SIDE - lanes, 1), pltpu.roll(value, lanes, 1))


def along_kernel(x_ref, coefs, out_ref, c_ref, s_ref):
    gather, scatter = gather_matrix(), scatter_matrix()
    a2, b2, a3, b3 = (coefs.at[pl.ds(16 * k, 16)] for k in range(4))
    spread = coefs[64:65]
    xh, xl = split(x_ref[...])
    c_ref[...] = dot(gather, xh) + dot(gather, xl)
    s_ref[:144] = swap_lanes(c_ref[:144], 32)
    s_ref[144:] = swap_lanes(c_ref[144:], 16)
    p2 = jnp.zeros((128, SIDE), F32)
    p3 = jnp.zeros((64, SIDE), F32)
    for t in range(TAPS):
        p2 = p2 + a2[t : t + 1] * c_ref[t : t + 128] + b2[t : t + 1] * s_ref[t : t + 128]
        p3 = p3 + a3[t : t + 1] * c_ref[144 + t : 208 + t] + b3[t : t + 1] * s_ref[144 + t : 208 + t]
    block = (lax.broadcasted_iota(jnp.int32, p3.shape, 1) // 16) % 4
    wide = jnp.where(block == 0, p3, jnp.where(block == 3, pltpu.roll(p3, 32, 1), pltpu.roll(p3, 16, 1)))
    wide = spread * wide
    both = jnp.concatenate([p2, wide, jnp.zeros((64, SIDE), F32)], 0)
    bh, bl = split(both)
    out_ref[...] = dot(scatter, bh) + dot(scatter, bl)


def along_z(received, coefs):
    return pl.pallas_call(
        along_kernel,
        out_shape=jax.ShapeDtypeStruct((COUNT * 16, SIDE), F32),
        scratch_shapes=[pltpu.VMEM((224, SIDE), F32), pltpu.VMEM((224, SIDE), F32)],
        compiler_params=params(),
        name="along",
        cost_estimate=pl.CostEstimate(flops=30000000, bytes_accessed=2000000, transcendentals=0),
    )(received, coefs)


def level_kernel(below, own, last, above, w_ref, p_ref):
    def cell_ref(c):
        ref, c = (below, c + 8) if c < 0 else (own, c) if c < 8 else (last, 7) if c == 8 else (above, c - 9)
        return ref, (3 + c // 4, c // 2 % 2, c % 2)

    def block(r, carry):
        rows = pl.ds(pl.multiple_of(8 * r, 8), 8)
        lower = pl.ds(pl.multiple_of(64 + 8 * r, 8), 8)
        for first, outputs in ((-1, 6), (5, 5)):
            def value(j):
                ref, i = cell_ref(first + j - REACH)
                return ref[(*i, rows)], ref[(*i, lower)]

            sums = slide(outputs, 1, value, lambda t: (w_ref[t, rows], w_ref[t, lower]))
            for i in range(outputs):
                p_ref[first + i + 1, rows] = sums[i][0]
                p_ref[first + i + 1, lower] = sums[i][1]
        return carry

    lax.fori_loop(0, 8, block, 0)


def level_one(below, own, last, above, w1):
    return pl.pallas_call(
        level_kernel,
        out_shape=jax.ShapeDtypeStruct((11, SIDE, SIDE), F32),
        compiler_params=params(),
        name="level",
        cost_estimate=pl.CostEstimate(flops=40000000, bytes_accessed=3000000, transcendentals=0),
    )(below, own, last, above, w1)


def spread_levels(level, y_ref, spread, out_ref, p_ref):
    lane = lax.broadcasted_iota(jnp.int32, (32, SIDE), 1)
    low = (lane // 32) % 2 == 0
    wides = []
    for c in range(9):
        y = y_ref[:, c, :]
        re = jnp.where(low, y, pltpu.roll(y, 32, 1))
        im = jnp.where(low, pltpu.roll(y, SIDE - 32, 1), y)
        wides.append((re, im))
    for c in range(-1, 10):
        for part in range(2):
            total = None
            for d, weight in CUBIC.items():
                if (c - d) % 2 == 0 and -2 <= (c - d) // 2 <= 6:
                    term = weight * wides[(c - d) // 2 + 2][part]
                    total = term if total is None else total + term
            for tile in range(2):
                rows = slice(64 * part + 32 * tile, 64 * part + 32 * tile + 32)
                p_ref[c + 1, rows] = level[c + 1, rows] + spread[32 * tile : 32 * tile + 32] * total
    for z in range(SLAB):
        total = None
        for d, weight in CUBIC.items():
            if (z - d) % 2 == 0:
                term = weight * p_ref[(z - d) // 2 + 1]
                total = term if total is None else total + term
        out_ref[z] = total


def sums_kernel(layers, groups, *refs):
    sources, w_ref, out = refs[:-2], refs[-2], refs[-1]
    for k, z in enumerate(groups):
        def block(r, carry):
            rows = pl.ds(pl.multiple_of(8 * r, 8), 8)

            def value(j):
                if z + j - REACH not in layers:
                    return None
                n, i = layers[z + j - REACH]
                return [sources[n][i, pair, part, rows] for pair in range(2) for part in range(2)]

            sums = slide(4, 2, value, lambda t: (w_ref[t, 0, rows], w_ref[t, 1, rows]))
            for i in range(4):
                for n in range(4):
                    out[4 * k + i, n // 2, n % 2, rows] = sums[i][n]
            return carry

        lax.fori_loop(0, SIDE // 8, block, 0)


def sums_along_z(pieces, layers, groups, w0):
    return pl.pallas_call(
        functools.partial(sums_kernel, layers, groups),
        out_shape=jax.ShapeDtypeStruct((4 * len(groups), 2, 2, SIDE, SIDE), F32),
        compiler_params=params(24),
        name="sums",
        cost_estimate=pl.CostEstimate(flops=100000000, bytes_accessed=9000000, transcendentals=0),
    )(*pieces, w0)


def finish_kernel(
    acc, near_low, near_high, far_low, far_high, w_ref, level, y_ref, small, spread, mats, out, coarse, p_ref, sum_ref
):
    step = pl.program_id(0)

    @pl.when(step == 0)
    def _():
        spread_levels(level, y_ref, small, coarse, p_ref)

    halo = [(far_low, k, k - 7) for k in range(4)] + [(near_low, k, k - 3) for k in range(3)]
    halo += [(near_high, k, 16 + k) for k in range(3)] + [(far_high, k, 19 + k) for k in range(4)]

    def add_halo(first):
        def block(r, carry):
            rows = pl.ds(pl.multiple_of(8 * r, 8), 8)
            for i in range(2):
                sums = [acc[i, pair, part, rows] for pair in range(2) for part in range(2)]
                for ref, k, z in halo:
                    t = z - first - i + REACH
                    if not 0 <= t < TAPS:
                        continue
                    wr, wi = w_ref[t, 0, rows], w_ref[t, 1, rows]
                    for pair in range(2):
                        vr, vi = ref[k, pair, 0, rows], ref[k, pair, 1, rows]
                        sums[2 * pair] += wr * vr - wi * vi
                        sums[2 * pair + 1] += wr * vi + wi * vr
                for n in range(4):
                    sum_ref[i, n // 2, n % 2, rows] = sums[n]
            return carry

        lax.fori_loop(0, SIDE // 8, block, 0)

    for number, first in enumerate((4, 6, 8, 10, 0, 2, 12, 14)):
        @pl.when(step == number)
        def _():
            add_halo(first)

    lane = lax.broadcasted_iota(jnp.int32, (64, SIDE), 1)
    z = 2 * pair_of_layers(step)

    columns = []
    for i in range(2):
        sides = [[], []]
        for part in range(2):
            g = coarse[z + i, 64 * part : 64 * part + 64]
            h = pltpu.roll(g, 64, 1)
            for pair in range(2):
                tile = jnp.where((lane < 64) == (pair == 0), g, h)
                for row in (0, 64):
                    sides[pair].append(sum_ref[i, pair, part, row : row + 64] + spread[row : row + 64] * tile)
        columns += [jnp.concatenate(side, 0) for side in sides]
    c = left_mul(mats[0], mats[1], jnp.concatenate(columns, 1))
    rows = jnp.concatenate(
        [
            jnp.concatenate([c[:SIDE, SIDE * n : SIDE * n + SIDE], c[SIDE:, SIDE * n : SIDE * n + SIDE]], 1)
            for n in range(4)
        ],
        0,
    )
    d = right_mul(rows, mats[2], mats[3])
    for n in range(4):
        for half in range(2):
            out[2 * (n % 2) + half, n // 2] = d[SIDE * n : SIDE * n + SIDE, SIDE * half : SIDE * half + SIDE]


def pair_of_layers(step):
    return jnp.where(step < 4, 2 + step, jnp.where(step < 6, step - 4, step))


def finish(acc, halos, w0, level, potentials, mats):
    full, half = spread_weights()
    return pl.pallas_call(
        finish_kernel,
        grid=(8,),
        in_specs=[
            pl.BlockSpec((2, 2, 2, SIDE, SIDE), lambda i: (pair_of_layers(i), 0, 0, 0, 0)),
            whole((5, 2, 2, SIDE, SIDE)),
            whole((5, 2, 2, SIDE, SIDE)),
            whole((4, 2, 2, SIDE, SIDE)),
            whole((4, 2, 2, SIDE, SIDE)),
            whole((TAPS, 2, SIDE, SIDE)),
            whole((11, SIDE, SIDE)),
            whole((COUNT, 16, SIDE)),
            whole((64, SIDE)),
            whole((SIDE, SIDE)),
            pl.BlockSpec((4, 256, 256), lambda i: (1, 0, 0)),
        ],
        out_specs=pl.BlockSpec((4, 2, SIDE, SIDE), lambda i: (0, pair_of_layers(i), 0, 0)),
        out_shape=jax.ShapeDtypeStruct((4, SLAB, SIDE, SIDE), F32),
        scratch_shapes=[
            pltpu.VMEM((SLAB, SIDE, SIDE), F32),
            pltpu.VMEM((11, SIDE, SIDE), F32),
            pltpu.VMEM((2, 2, 2, SIDE, SIDE), F32),
        ],
        compiler_params=params(28),
        name="finish",
        cost_estimate=pl.CostEstimate(flops=3000000000, bytes_accessed=10000000, transcendentals=0),
    )(acc, *halos, w0, level, potentials, jnp.asarray(half), jnp.asarray(full), mats)


def slide(outputs, pairs, value, weight):
    sums = [[None] * (2 * pairs) for _ in range(outputs)]
    window = {}
    for j in range(outputs + TAPS - 1):
        if j < TAPS:
            window[j] = weight(j)
        v = value(j)
        for i in range(outputs if v is not None else 0):
            t = j - i
            if not 0 <= t < TAPS:
                continue
            wr, wi = window[t]
            for pair in range(pairs):
                vr, vi = v[2 * pair], v[2 * pair + 1]
                for k, term in ((2 * pair, wr * vr - wi * vi), (2 * pair + 1, wr * vi + wi * vr)):
                    sums[i][k] = term if sums[i][k] is None else sums[i][k] + term
    return sums


def shifted(value, steps):
    pairs = [(source, (source + steps) % COUNT) for source in range(COUNT)]
    return lax.ppermute(value, "space", pairs)


def wave_table():
    columns = []
    for side in (128, 64, 32, 16):
        offset = np.arange(SIDE) % max(side, 64)
        lanes = np.where(offset < 2 * side, offset % side, -1)
        angle = 2.0 * np.pi * np.outer(np.arange(TAPS) - REACH, lanes) / side
        columns += [np.where(lanes >= 0, np.cos(angle), 0.0), np.where(lanes >= 0, np.sin(angle), 0.0)]
    return np.concatenate(columns, 1).astype(np.float32)


def modes_kernel(me_ref, taps_ref, rows_ref, cols_ref, z_ref, w0_ref, w1_ref, coef_ref):
    def row(level, term, dim, part):
        return rows_ref[pl.ds((level * 4 + term) * 3 + dim, 1), pl.ds((2 * level + part) * SIDE, SIDE)]

    for level, w_ref, side in ((0, w0_ref, 128), (1, w1_ref, 64)):
        for block in range(0, side, 32):
            real, imag = [], []
            for term in range(4):
                column = (level * 4 + term) * 3 + 1
                yr = cols_ref[pl.ds(2 * level * SIDE + block, 32), pl.ds(column, 1)]
                yi = cols_ref[pl.ds((2 * level + 1) * SIDE + block, 32), pl.ds(column, 1)]
                xr, xi = row(level, term, 2, 0), row(level, term, 2, 1)
                real.append(yr * xr - yi * xi)
                imag.append(yr * xi + yi * xr)

            def tap(t, carry):
                for part, values in ((0, real), (1, imag)):
                    total = None
                    for term in range(4):
                        scaled = taps_ref[(level * 4 + term) * TAPS + t] * values[term]
                        total = scaled if total is None else total + scaled
                    w_ref[t, pl.ds(part * side + block, 32)] = total
                return carry

            lax.fori_loop(0, TAPS, tap, 0)

    me = me_ref[0]
    coef_ref[...] = jnp.zeros_like(coef_ref)
    for level, base, side in ((2, 0, 32), (3, 32, 16)):
        lane = lax.broadcasted_iota(jnp.int32, (1, SIDE), 1)
        sign = jnp.where((lane // side) % 2 == 0, -1.0, 1.0)
        chosen = lane == lax.rem(me, side)
        a = b = None
        for term in range(4):
            yr = jnp.sum(jnp.where(chosen, row(level, term, 1, 0), 0.0), axis=1, keepdims=True)
            yi = jnp.sum(jnp.where(chosen, row(level, term, 1, 1), 0.0), axis=1, keepdims=True)
            xr, xi = row(level, term, 2, 0), row(level, term, 2, 1)
            z = z_ref[:, pl.ds(level * 4 + term, 1)]
            ta = z * (yr * xr - yi * xi)
            tb = z * (sign * (yr * xi + yi * xr))
            a = ta if a is None else a + ta
            b = tb if b is None else b + tb
        coef_ref[pl.ds(base, TAPS)] = a
        coef_ref[pl.ds(base + 16, TAPS)] = b
    lane = lax.broadcasted_iota(jnp.int32, (1, SIDE), 1)
    theta = (lane % 32).astype(F32) * (2.0 * np.pi / 32)
    symbols = 1.0 + 1.125 * jnp.cos(theta) - 0.125 * jnp.cos(3.0 * theta)
    chosen = jnp.sum(jnp.where(lane == me, symbols, 0.0), axis=1, keepdims=True)
    coef_ref[pl.ds(64, 1)] = symbols * chosen


def kernel_modes(taps, me):
    table = jnp.asarray(wave_table())
    flat = taps.reshape(48, TAPS)
    z = taps[:, :, 0].reshape(16, TAPS)
    exact = lax.Precision.HIGHEST
    rows = jnp.dot(flat, table, precision=exact)
    cols = jnp.dot(jnp.asarray(wave_table().T), flat.T, precision=exact)
    outs = [(TAPS, 256, SIDE), (TAPS, SIDE, SIDE), (80, SIDE)]
    in_smem = pl.BlockSpec(memory_space=pltpu.SMEM)
    in_vmem = pl.BlockSpec(memory_space=pltpu.VMEM)
    return pl.pallas_call(
        modes_kernel,
        in_specs=[in_smem, in_smem, in_vmem, in_vmem, in_vmem],
        out_shape=[jax.ShapeDtypeStruct(s, F32) for s in outs],
        compiler_params=params(),
        name="modes",
        cost_estimate=pl.CostEstimate(flops=8000000, bytes_accessed=4000000, transcendentals=0),
    )(me.reshape(1), z.reshape(-1), rows, cols, z.T)


def body(charges, kernel_taps):
    mats = jnp.asarray(dft_parts())
    charges = pltpu.with_memory_space_constraint(charges, pltpu.HBM)
    me = lax.axis_index("space")

    to_above, to_below, own, payload = partial_sums(charges)
    from_below = shifted(to_above, 1)
    from_above = shifted(to_below, -1)
    received = lax.all_to_all(payload, "space", 0, 0, tiled=True)

    near_down, near_up = near_layers(charges, mats, own, from_below, from_above, own)
    near_lower, near_upper = shifted(near_up, 1), shifted(near_down, -1)
    far_down, far_up, low_mid, high_mid = far_layers(charges, mats, near_up)
    far_lower, far_upper = shifted(far_up, 1), shifted(far_down, -1)

    w0, w1, coefs = kernel_modes(kernel_taps, me)
    w0 = w0.reshape(TAPS, 2, SIDE, SIDE)

    spread_out = along_z(received.reshape(COUNT * 16, SIDE), coefs)
    potentials = lax.all_to_all(spread_out.reshape(COUNT, 16, SIDE), "space", 0, 0, tiled=True)

    pieces = (near_down, far_down, low_mid, high_mid, far_up, near_up)
    places = ((0, 3), (3, 4), (7, 1), (8, 1), (9, 4), (13, 3))
    layers = {first + i: (k, i) for k, (first, count) in enumerate(places) for i in range(count)}
    acc = sums_along_z(pieces, layers, (0, 4, 8, 12), w0)
    acc = pltpu.with_memory_space_constraint(acc, pltpu.HBM)
    level = level_one(near_lower, near_up, near_down, near_upper, w1)
    return finish(acc, (near_lower, near_upper, far_lower, far_upper), w0, level, potentials, mats)


def solution(mesh):
    placed = (P("bead", "space", None, None), P())
    return jax.shard_map(
        body, mesh=mesh, in_specs=placed, out_specs=P("bead", "space", None, None), check_vma=False
    )
```

profile of v0, /device:TPU:2, one launch (start us, length us, event | category | flops | bytes accessed | tf_op | source)
XLA Modules:
  0.0 137.8 jit_solution(13985247428862811898)
XLA Ops:
  0.0 1.0 copy-done.9
  1.0 0.8 copy-done.11
  1.8 7.9 %partial.1 = (f32[2,128,128]{2,1,0:T(8,128)S(1)}, f32[2,128,128]{2,1,0:T(8,128)S(1)}, f32[9,128,128]{2,1,0:T(8,128)S(1)}, f32[32,16,128]{2,1,0:T(8,128)}) custom-call(f32[4,16,128,128]{3,2,1,0:T(8,128)} %v_high.3, bf16[512,256]{1,0:T(8,128)(2,1)S(1)} %copy-done.9, f32[96,128]{1,0:T(8,128)S(1)} %copy-done.11), custom_call_target="tpu_custom_call" | custom-call | flops 500000000 | bytes 6000000 | tf_op jit(solution)/shard_map/partial/pallas_call | solution.py:277
  9.8 1.7 %collective-permute-start = (f32[2,128,128]{2,1,0:T(8,128)S(1)}, f32[2,128,128]{2,1,0:T(8,128)S(1)}, u32[]{:S(2)}, u32[]{:S(2)}) collective-permute-start(f32[2,128,128]{2,1,0:T(8,128)S(1)} %get-tuple-element.19), channel_id=1, source_target_pairs={{0,1},{1,2},{2,3},{3,4},{4,5},{5,6},{6,7},{7,8},{8,9},{9,10},{10,1... | collective-permute-start | bytes 393224 | tf_op jit(solution)/shard_map/ppermute | solution.py:568
  11.4 6.8 %collective-permute-start.1 = (f32[2,128,128]{2,1,0:T(8,128)S(1)}, f32[2,128,128]{2,1,0:T(8,128)S(1)}, u32[]{:S(2)}, u32[]{:S(2)}) collective-permute-start(f32[2,128,128]{2,1,0:T(8,128)S(1)} %get-tuple-element.20), channel_id=1, source_target_pairs={{0,31},{1,0},{2,1},{3,2},{4,3},{5,4},{6,5},{7,6},{8,7},{9,8},{10,9... | collective-permute-start | bytes 393224 | tf_op jit(solution)/shard_map/ppermute | solution.py:568
  18.2 3.4 %collective-permute-done.from_below = f32[2,128,128]{2,1,0:T(8,128)S(1)} collective-permute-done((f32[2,128,128]{2,1,0:T(8,128)S(1)}, f32[2,128,128]{2,1,0:T(8,128)S(1)}, u32[]{:S(2)}, u32[]{:S(2)}) %collective-permute-start) | collective-permute-done | bytes 131104 | tf_op jit(solution)/shard_map/ppermute | solution.py:568
  21.7 0.0 collective-permute-done.1.from_above
  21.7 0.0 copy-done.1
  21.7 5.6 %near.1 = (f32[5,2,2,128,128]{4,3,2,1,0:T(8,128)}, f32[5,2,2,128,128]{4,3,2,1,0:T(8,128)S(1)}) custom-call(f32[4,16,128,128]{3,2,1,0:T(8,128)} %v_high.3, f32[4,16,128,128]{3,2,1,0:T(8,128)} %v_high.3, bf16[8,256,256]{2,1,0:T(8,128)(2,1)S(1)} %copy-done.1, f32[9,128,128]{2,1,0:T(8,128)S(1)} %get-tuple-element.18.own.token, ...), custom_call_target="tpu_custom_call" | custom-call | flops 1200000000 | bytes 5000000 | tf_op jit(solution)/shard_map/near/pallas_call | solution.py:138
  27.3 5.1 %collective-permute-start.3 = (f32[5,2,2,128,128]{4,3,2,1,0:T(8,128)}, f32[5,2,2,128,128]{4,3,2,1,0:T(8,128)}, u32[]{:S(2)}, u32[]{:S(2)}) collective-permute-start(f32[5,2,2,128,128]{4,3,2,1,0:T(8,128)} %get-tuple-element.21.refs_0_.last), channel_id=1, source_target_pairs={{0,31},{1,0},{2,1},{3,2},{4,3},{5,4},{6,5},{7,6},{8,7},{9,8},{10,9... | collective-permute-start | bytes 3932168 | tf_op jit(solution)/shard_map/ppermute | solution.py:568
  32.4 0.0 collective-permute-start.2
  32.4 7.1 %far.1 = (f32[4,2,2,128,128]{4,3,2,1,0:T(8,128)}, f32[4,2,2,128,128]{4,3,2,1,0:T(8,128)}, f32[1,2,2,128,128]{4,3,2,1,0:T(8,128)S(1)}, f32[1,2,2,128,128]{4,3,2,1,0:T(8,128)S(1)}) custom-call(f32[4,16,128,128]{3,2,1,0:T(8,128)} %v_high.3, f32[4,16,128,128]{3,2,1,0:T(8,128)} %v_high.3, bf16[8,256,256]{2,1,0:T(8,128)(2,1)S(1)} %copy-done.1, ...), custom_call_target="tpu_custom_call" | custom-call | flops 2000000000 | bytes 6000000 | tf_op jit(solution)/shard_map/far/pallas_call | solution.py:177
  39.5 0.7 copy-done.7
  40.2 5.3 %collective-permute-start.5 = (f32[4,2,2,128,128]{4,3,2,1,0:T(8,128)}, f32[4,2,2,128,128]{4,3,2,1,0:T(8,128)}, u32[]{:S(2)}, u32[]{:S(2)}) collective-permute-start(f32[4,2,2,128,128]{4,3,2,1,0:T(8,128)} %get-tuple-element.23.refs_1_), channel_id=1, source_target_pairs={{0,31},{1,0},{2,1},{3,2},{4,3},{5,4},{6,5},{7,6},{8,7},{9,8},{10,9... | collective-permute-start | bytes 3145736 | tf_op jit(solution)/shard_map/ppermute | solution.py:568
  45.4 0.0 collective-permute-start.4
  45.4 8.4 %all-to-all-start = ((f32[32,16,128]{2,1,0:T(8,128)}), f32[32,16,128]{2,1,0:T(8,128)S(1)}, u32[]{:S(2)}, u32[]{:S(2)}) async-start(f32[32,16,128]{2,1,0:T(8,128)} %get-tuple-element.29), calls=%async_computation | async-start | bytes 524288 | tf_op jit(solution)/shard_map/all_to_all | solution.py:660
  53.9 0.0 copy-done.14
  53.9 0.1 reshape_reshape_squeeze.3.taps_ref
  54.0 0.1 copy.13
  54.1 1.1 convolution_bitcast_fusion.rows_ref
  55.2 0.0 copy-done.13
  55.2 0.6 fusion.cols_ref
  55.8 2.9 %modes.1 = (f32[15,256,128]{2,1,0:T(8,128)S(1)}, f32[15,128,128]{2,1,0:T(8,128)S(1)}, f32[80,128]{1,0:T(8,128)S(1)}) custom-call(s32[1]{0:T(128)} %bitcast.me_ref, f32[240]{0:T(256)S(1)} %reshape_reshape_squeeze.3.taps_ref, f32[48,1024]{1,0:T(8,128)S(1)} %convolution_bitcast_fusion.rows_ref, f32[1024,48]{1,0:T(8,128)S(1)} %fusion.cols_ref, f32[15,16]{1,0:T(8,128)S(1)} %bitcast.17), custom_call_target="tpu_custom_call" | custom-call | flops 8000000 | bytes 4000000 | tf_op jit(solution)/shard_map/modes/pallas_call | solution.py:642
  58.7 1.3 copy-done.2
  60.0 1.0 copy-done.5
  61.0 33.4 %all-to-all-done = f32[32,16,128]{2,1,0:T(8,128)S(1)} async-done(((f32[32,16,128]{2,1,0:T(8,128)}), f32[32,16,128]{2,1,0:T(8,128)S(1)}, u32[]{:S(2)}, u32[]{:S(2)}) %all-to-all-start) | async-done | bytes 262176 | tf_op jit(solution)/shard_map/all_to_all | solution.py:660
  94.3 1.9 %along.1 = f32[512,128]{1,0:T(8,128)} custom-call(f32[512,128]{1,0:T(8,128)S(1)} %bitcast.16, f32[80,128]{1,0:T(8,128)S(1)} %get-tuple-element.30.coefs), custom_call_target="tpu_custom_call" | custom-call | flops 30000000 | bytes 2000000 | tf_op jit(solution)/shard_map/along/pallas_call | solution.py:346
  96.3 6.5 %all-to-all-start.1 = ((f32[32,16,128]{2,1,0:T(8,128)}), f32[32,16,128]{2,1,0:T(8,128)S(1)}, u32[]{:S(2)}, u32[]{:S(2)}) async-start(f32[32,16,128]{2,1,0:T(8,128)} %bitcast.6), calls=%async_computation.1 | async-start | bytes 524288 | tf_op jit(solution)/shard_map/all_to_all | solution.py:671
  102.8 0.0 copy-start.3
  102.8 1.5 %copy-done.3 = f32[15,256,128]{2,1,0:T(8,128)S(1)} copy-done((f32[15,256,128]{2,1,0:T(8,128)S(1)}, f32[15,256,128]{2,1,0:T(8,128)}, u32[]{:S(2)}) %copy-start.3) | copy-done | bytes 1966104
  104.3 0.9 copy-done.8
  105.3 10.5 %sums.1.acc = f32[16,2,2,128,128]{4,3,2,1,0:T(8,128)S(1)} custom-call(f32[5,2,2,128,128]{4,3,2,1,0:T(8,128)} %get-tuple-element.21.refs_0_.last, f32[4,2,2,128,128]{4,3,2,1,0:T(8,128)} %get-tuple-element.23.refs_1_, f32[1,2,2,128,128]{4,3,2,1,0:T(8,128)S(1)} %get-tuple-element.24.refs_2_, f32[1,2,2,128,128]{4,3,2,1,0:T(8,128)S(1)} %copy-done.8, ...), custom_call_target="tpu_custom_call" | custom-call | flops 100000000 | bytes 9000000 | tf_op jit(solution)/shard_map/sums/pallas_call | solution.py:438
  115.8 0.0 copy-start
  115.8 1.9 %copy-done = f32[16,2,2,128,128]{4,3,2,1,0:T(8,128)} copy-done((f32[16,2,2,128,128]{4,3,2,1,0:T(8,128)}, f32[16,2,2,128,128]{4,3,2,1,0:T(8,128)S(1)}, u32[]{:S(2)}) %copy-start) | copy-done | bytes 4194328
  117.7 0.0 collective-permute-done.3.above.near_high
  117.7 0.0 collective-permute-done.2.below.near_low
  117.7 0.0 copy-done.6
  117.7 0.0 copy-start.10
  117.8 0.0 copy-start.12
  117.8 4.0 %level.1 = f32[11,128,128]{2,1,0:T(8,128)S(1)} custom-call(f32[5,2,2,128,128]{4,3,2,1,0:T(8,128)} %collective-permute-done.2.below.near_low, f32[5,2,2,128,128]{4,3,2,1,0:T(8,128)S(1)} %get-tuple-element.22.token.refs_5_.own, f32[5,2,2,128,128]{4,3,2,1,0:T(8,128)} %get-tuple-element.21.refs_0_.last, ...), custom_call_target="tpu_custom_call" | custom-call | flops 40000000 | bytes 3000000 | tf_op jit(solution)/shard_map/level/pallas_call | solution.py:379
  121.8 0.0 all-to-all-done.1.y_ref
  121.8 0.0 collective-permute-done.5.far_high
  121.8 0.0 collective-permute-done.4.far_low
  121.8 0.0 copy-done.10
  121.8 0.0 copy-done.12
  121.9 0.0 copy-start.4
  121.9 1.5 %copy-done.4 = f32[15,256,128]{2,1,0:T(8,128)S(1)} copy-done((f32[15,256,128]{2,1,0:T(8,128)S(1)}, f32[15,256,128]{2,1,0:T(8,128)}, u32[]{:S(2)}) %copy-start.4) | copy-done | bytes 1966104
  123.4 14.4 %finish.1 = f32[4,16,128,128]{3,2,1,0:T(8,128)} custom-call(f32[16,2,2,128,128]{4,3,2,1,0:T(8,128)} %copy-done, f32[5,2,2,128,128]{4,3,2,1,0:T(8,128)} %collective-permute-done.2.below.near_low, f32[5,2,2,128,128]{4,3,2,1,0:T(8,128)} %collective-permute-done.3.above.near_high, f32[4,2,2,128,128]{4,3,2,1,0:T(8,128)} %collective-permute-done.4.far_low, ...), custom_call_target="tpu_custom_call" | custom-call | flops 3000000000 | bytes 10000000 | tf_op jit(solution)/shard_map/finish/pallas_call | solution.py:518
  (13 shorter events, 0.0 us)
Async XLA Ops:
  0.0 21.7 %copy-start.1 = (bf16[8,256,256]{2,1,0:T(8,128)(2,1)S(1)}, bf16[8,256,256]{2,1,0:T(8,128)(2,1)}, u32[]{:S(2)}) copy-start(bf16[8,256,256]{2,1,0:T(8,128)(2,1)} %constant.18.clone.mats) | copy-start | bytes 3145732
  0.0 1.0 copy-start.9
  1.0 0.8 copy-start.11
  9.8 11.9 %collective-permute-start = (f32[2,128,128]{2,1,0:T(8,128)S(1)}, f32[2,128,128]{2,1,0:T(8,128)S(1)}, u32[]{:S(2)}, u32[]{:S(2)}) collective-permute-start(f32[2,128,128]{2,1,0:T(8,128)S(1)} %get-tuple-element.19), channel_id=1, source_target_pairs={{0,1},{1,2},{2,3},{3,4},{4,5},{5,6},{6,7},{7,8},{8,9},{9,10},{10,1... | collective-permute-start | bytes 393224 | tf_op jit(solution)/shard_map/ppermute | solution.py:568
  11.4 10.2 %collective-permute-start.1 = (f32[2,128,128]{2,1,0:T(8,128)S(1)}, f32[2,128,128]{2,1,0:T(8,128)S(1)}, u32[]{:S(2)}, u32[]{:S(2)}) collective-permute-start(f32[2,128,128]{2,1,0:T(8,128)S(1)} %get-tuple-element.20), channel_id=1, source_target_pairs={{0,31},{1,0},{2,1},{3,2},{4,3},{5,4},{6,5},{7,6},{8,7},{9,8},{10,9... | collective-permute-start | bytes 393224 | tf_op jit(solution)/shard_map/ppermute | solution.py:568
  27.3 90.5 %collective-permute-start.3 = (f32[5,2,2,128,128]{4,3,2,1,0:T(8,128)}, f32[5,2,2,128,128]{4,3,2,1,0:T(8,128)}, u32[]{:S(2)}, u32[]{:S(2)}) collective-permute-start(f32[5,2,2,128,128]{4,3,2,1,0:T(8,128)} %get-tuple-element.21.refs_0_.last), channel_id=1, source_target_pairs={{0,31},{1,0},{2,1},{3,2},{4,3},{5,4},{6,5},{7,6},{8,7},{9,8},{10,9... | collective-permute-start | bytes 3932168 | tf_op jit(solution)/shard_map/ppermute | solution.py:568
  32.4 21.5 %copy-start.14 = (f32[4,4,3,15]{3,1,2,0:T(4,128)S(1)}, f32[4,4,3,15]{3,1,2,0:T(4,128)}, u32[]{:S(2)}) copy-start(f32[4,4,3,15]{3,1,2,0:T(4,128)} %param.10) | copy-start | bytes 8644
  32.4 22.9 %copy-start.13 = (f32[1024,15]{1,0:T(8,128)S(1)}, f32[1024,15]{1,0:T(8,128)}, u32[]{:S(2)}) copy-start(f32[1024,15]{1,0:T(8,128)} %constant.22.clone) | copy-start | bytes 184324
  32.4 85.3 %collective-permute-start.2 = (f32[5,2,2,128,128]{4,3,2,1,0:T(8,128)S(1)}, f32[5,2,2,128,128]{4,3,2,1,0:T(8,128)}, u32[]{:S(2)}, u32[]{:S(2)}) collective-permute-start(f32[5,2,2,128,128]{4,3,2,1,0:T(8,128)S(1)} %get-tuple-element.22.token.refs_5_.own), channel_id=1, source_target_pairs={{0,1},{1,2},{2,3},{3,4},{4,5},{5,6},{6,7},{7,8},{8,9},{9,10},{10,1... | collective-permute-start | bytes 3932168 | tf_op jit(solution)/shard_map/ppermute | solution.py:568
  39.5 0.7 copy-start.7
  40.2 81.6 %collective-permute-start.5 = (f32[4,2,2,128,128]{4,3,2,1,0:T(8,128)}, f32[4,2,2,128,128]{4,3,2,1,0:T(8,128)}, u32[]{:S(2)}, u32[]{:S(2)}) collective-permute-start(f32[4,2,2,128,128]{4,3,2,1,0:T(8,128)} %get-tuple-element.23.refs_1_), channel_id=1, source_target_pairs={{0,31},{1,0},{2,1},{3,2},{4,3},{5,4},{6,5},{7,6},{8,7},{9,8},{10,9... | collective-permute-start | bytes 3145736 | tf_op jit(solution)/shard_map/ppermute | solution.py:568
  45.4 76.4 %collective-permute-start.4 = (f32[4,2,2,128,128]{4,3,2,1,0:T(8,128)}, f32[4,2,2,128,128]{4,3,2,1,0:T(8,128)}, u32[]{:S(2)}, u32[]{:S(2)}) collective-permute-start(f32[4,2,2,128,128]{4,3,2,1,0:T(8,128)} %get-tuple-element.26.refs_4_), channel_id=1, source_target_pairs={{0,1},{1,2},{2,3},{3,4},{4,5},{5,6},{6,7},{7,8},{8,9},{9,10},{10,1... | collective-permute-start | bytes 3145736 | tf_op jit(solution)/shard_map/ppermute | solution.py:568
  45.4 48.9 %all-to-all-start = ((f32[32,16,128]{2,1,0:T(8,128)}), f32[32,16,128]{2,1,0:T(8,128)S(1)}, u32[]{:S(2)}, u32[]{:S(2)}) async-start(f32[32,16,128]{2,1,0:T(8,128)} %get-tuple-element.29), calls=%async_computation | async-start | bytes 524288 | tf_op jit(solution)/shard_map/all_to_all | solution.py:660
  58.7 1.3 copy-start.2
  60.0 1.0 copy-start.5
  96.3 25.5 %all-to-all-start.1 = ((f32[32,16,128]{2,1,0:T(8,128)}), f32[32,16,128]{2,1,0:T(8,128)S(1)}, u32[]{:S(2)}, u32[]{:S(2)}) async-start(f32[32,16,128]{2,1,0:T(8,128)} %bitcast.6), calls=%async_computation.1 | async-start | bytes 524288 | tf_op jit(solution)/shard_map/all_to_all | solution.py:671
  102.8 1.5 %copy-start.3 = (f32[15,256,128]{2,1,0:T(8,128)S(1)}, f32[15,256,128]{2,1,0:T(8,128)}, u32[]{:S(2)}) copy-start(f32[15,256,128]{2,1,0:T(8,128)} %copy-done.2) | copy-start | bytes 5898244
  104.3 0.9 copy-start.8
  105.3 12.5 %copy-start.6 = (f32[15,128,128]{2,1,0:T(8,128)S(1)}, f32[15,128,128]{2,1,0:T(8,128)}, u32[]{:S(2)}) copy-start(f32[15,128,128]{2,1,0:T(8,128)} %copy-done.5) | copy-start | bytes 2949124
  115.8 1.9 %copy-start = (f32[16,2,2,128,128]{4,3,2,1,0:T(8,128)}, f32[16,2,2,128,128]{4,3,2,1,0:T(8,128)S(1)}, u32[]{:S(2)}) copy-start(f32[16,2,2,128,128]{4,3,2,1,0:T(8,128)S(1)} %sums.1.acc) | copy-start | bytes 12582916
  117.7 4.1 %copy-start.10 = (f32[128,128]{1,0:T(8,128)S(1)}, f32[128,128]{1,0:T(8,128)}, u32[]{:S(2)}) copy-start(f32[128,128]{1,0:T(8,128)} %constant.24.clone.spread) | copy-start | bytes 196612
  117.8 4.1 %copy-start.12 = (f32[64,128]{1,0:T(8,128)S(1)}, f32[64,128]{1,0:T(8,128)}, u32[]{:S(2)}) copy-start(f32[64,128]{1,0:T(8,128)} %constant.23.clone.small) | copy-start | bytes 98308
  121.9 1.5 %copy-start.4 = (f32[15,256,128]{2,1,0:T(8,128)S(1)}, f32[15,256,128]{2,1,0:T(8,128)}, u32[]{:S(2)}) copy-start(f32[15,256,128]{2,1,0:T(8,128)} %copy-done.2) | copy-start | bytes 5898244
where the time goes:
time: 139 us; the launch traced here: 138 us
  Pallas kernels  54.4 us (39%)
  waiting for transfers between devices  36.8 us (26%)
  starting transfers between devices  33.8 us (24%)
  local copies, waits for them, and re-layouts  11 us (8%)
  matrix products  1.71 us (1%)
    all_to_all x1, waiting for transfers between devices, body(): received = lax.all_to_all(payload, 'space', 0, 0, tiled=True)  33.4 us
    ppermute x6, starting transfers between devices, shifted(): return lax.ppermute(value, 'space', pairs)  18.9 us
    pallas_call x1, Pallas kernels, finish(): pl.pallas_call(finish_kernel, grid=(8,), in_specs=[pl.BlockSpec((2, 2, 2,...  14.4 us
    unnamed x31, local copies, waits for them, and re-layouts  10.8 us
    pallas_call x1, Pallas kernels, sums_along_z(): pl.pallas_call(functools.partial(sums_kernel, layers, groups), out_shape=...  10.5 us
    all_to_all x1, starting transfers between devices, body(): received = lax.all_to_all(payload, 'space', 0, 0, tiled=True)  8.39 us
    pallas_call x1, Pallas kernels, partial_sums(): pl.pallas_call(partial_kernel, out_shape=[jax.ShapeDtypeStruct(s, F32) fo...  7.93 us
    pallas_call x1, Pallas kernels, far_layers(): pl.pallas_call(far_kernel, grid=(5,), in_specs=[pl.BlockSpec((4, 1, SIDE,...  7.09 us
  transfers between devices with their start and end apart: 8, of which 2 were waited for; matrix products, arithmetic and copies ran while one was open for 1% of the time, Pallas kernels for 19%

commit v1 on v0

--- a/solution.py
+++ b/solution.py
@@ -151,7 +151,7 @@
         out_shape=[shape, shape],
         compiler_params=params(),
         name="near",
-        cost_estimate=pl.CostEstimate(flops=1200000000, bytes_accessed=5000000, transcendentals=0),
+        cost_estimate=pl.CostEstimate(flops=1000, bytes_accessed=1000, transcendentals=0),
     )(charges, charges, mats, own, from_below, from_above, token)
 
 
@@ -187,7 +187,7 @@
         out_shape=[shape, shape, single, single],
         compiler_params=params(),
         name="far",
-        cost_estimate=pl.CostEstimate(flops=2000000000, bytes_accessed=6000000, transcendentals=0),
+        cost_estimate=pl.CostEstimate(flops=1000, bytes_accessed=1000, transcendentals=0),
     )(charges, charges, mats, token)
 
 
@@ -289,7 +289,7 @@
         ],
         compiler_params=params(),
         name="partial",
-        cost_estimate=pl.CostEstimate(flops=500000000, bytes_accessed=6000000, transcendentals=0),
+        cost_estimate=pl.CostEstimate(flops=1000, bytes_accessed=1000, transcendentals=0),
     )(charges, jnp.asarray(coarse_parts()), jnp.asarray(fold_weights()))
 
 
@@ -349,7 +349,7 @@
         scratch_shapes=[pltpu.VMEM((224, SIDE), F32), pltpu.VMEM((224, SIDE), F32)],
         compiler_params=params(),
         name="along",
-        cost_estimate=pl.CostEstimate(flops=30000000, bytes_accessed=2000000, transcendentals=0),
+        cost_estimate=pl.CostEstimate(flops=100000000000, bytes_accessed=400000000, transcendentals=0),
     )(received, coefs)
 
 
@@ -381,7 +381,7 @@
         out_shape=jax.ShapeDtypeStruct((11, SIDE, SIDE), F32),
         compiler_params=params(),
         name="level",
-        cost_estimate=pl.CostEstimate(flops=40000000, bytes_accessed=3000000, transcendentals=0),
+        cost_estimate=pl.CostEstimate(flops=1000, bytes_accessed=1000, transcendentals=0),
     )(below, own, last, above, w1)
 
 
@@ -440,7 +440,7 @@
         out_shape=jax.ShapeDtypeStruct((4 * len(groups), 2, 2, SIDE, SIDE), F32),
         compiler_params=params(24),
         name="sums",
-        cost_estimate=pl.CostEstimate(flops=100000000, bytes_accessed=9000000, transcendentals=0),
+        cost_estimate=pl.CostEstimate(flops=1000, bytes_accessed=1000, transcendentals=0),
     )(*pieces, w0)
 
 
@@ -540,7 +540,7 @@
         ],
         compiler_params=params(28),
         name="finish",
-        cost_estimate=pl.CostEstimate(flops=3000000000, bytes_accessed=10000000, transcendentals=0),
+        cost_estimate=pl.CostEstimate(flops=1000, bytes_accessed=1000, transcendentals=0),
     )(acc, *halos, w0, level, potentials, jnp.asarray(half), jnp.asarray(full), mats)
 
 
@@ -645,7 +645,7 @@
         out_shape=[jax.ShapeDtypeStruct(s, F32) for s in outs],
         compiler_params=params(),
         name="modes",
-        cost_estimate=pl.CostEstimate(flops=8000000, bytes_accessed=4000000, transcendentals=0),
+        cost_estimate=pl.CostEstimate(flops=1000, bytes_accessed=1000, transcendentals=0),
     )(me.reshape(1), z.reshape(-1), rows, cols, z.T)
 
 
@@ -659,9 +659,7 @@
     from_above = shifted(to_below, -1)
     received = lax.all_to_all(payload, "space", 0, 0, tiled=True)
 
-    near_down, near_up = near_layers(charges, mats, own, from_below, from_above, own)
-    near_lower, near_upper = shifted(near_up, 1), shifted(near_down, -1)
-    far_down, far_up, low_mid, high_mid = far_layers(charges, mats, near_up)
+    far_down, far_up, low_mid, high_mid = far_layers(charges, mats, own)
     far_lower, far_upper = shifted(far_up, 1), shifted(far_down, -1)
 
     w0, w1, coefs = kernel_modes(kernel_taps, me)
@@ -669,6 +667,9 @@
 
     spread_out = along_z(received.reshape(COUNT * 16, SIDE), coefs)
     potentials = lax.all_to_all(spread_out.reshape(COUNT, 16, SIDE), "space", 0, 0, tiled=True)
+
+    near_down, near_up = near_layers(charges, mats, own, from_below, from_above, spread_out)
+    near_lower, near_upper = shifted(near_up, 1), shifted(near_down, -1)
 
     pieces = (near_down, far_down, low_mid, high_mid, far_up, near_up)
     places = ((0, 3), (3, 4), (7, 1), (8, 1), (9, 4), (13, 3))

time: 139 us -> 123 us (0.88)
  waiting for transfers between devices: 36.8 us -> 24.7 us
  starting transfers between devices: 33.8 us -> 30.4 us
    all_to_all x1, waiting for transfers between devices: 33.4 us -> 2.79 us  [body(): received = lax.all_to_all(payload, 'space', 0, 0, tiled=True)]
    all_to_all x1, waiting for transfers between devices: 0.01 us -> 19.5 us  [body(): lax.all_to_all(spread_out.reshape(COUNT, 16, SIDE), 'space', 0, 0, tiled=...]
    ppermute x6, starting transfers between devices: 18.9 us -> 11 us  [shifted(): return lax.ppermute(value, 'space', pairs)]
    all_to_all x1, starting transfers between devices: 8.39 us -> 11.5 us  [body(): received = lax.all_to_all(payload, 'space', 0, 0, tiled=True)]
    all_to_all x1, starting transfers between devices: 6.5 us -> 7.93 us  [body(): lax.all_to_all(spread_out.reshape(COUNT, 16, SIDE), 'space', 0, 0, tiled=...]
    unnamed x31 -> x39, local copies, waits for them, and re-layouts: 10.8 us -> 10.6 us
  transfers between devices with their start and end apart: 8 -> 8, of which waited for: 2 -> 3; matrix products, arithmetic and copies ran while one was open for 1% -> 1% of each run, Pallas kernels for 19% -> 22%
where the time goes in v1:
time: 123 us; the launch traced here: 122 us
  Pallas kernels  55.5 us (45%)
  starting transfers between devices  30.4 us (25%)
  waiting for transfers between devices  24.7 us (20%)
  local copies, waits for them, and re-layouts  10.8 us (9%)
    all_to_all x1, waiting for transfers between devices, body(): lax.all_to_all(spread_out.reshape(COUNT, 16, SIDE), 'space', 0, 0, tiled=...  19.5 us
    pallas_call x1, Pallas kernels, finish(): pl.pallas_call(finish_kernel, grid=(8,), in_specs=[pl.BlockSpec((2, 2, 2,...  14.4 us
    all_to_all x1, starting transfers between devices, body(): received = lax.all_to_all(payload, 'space', 0, 0, tiled=True)  11.5 us
    ppermute x6, starting transfers between devices, shifted(): return lax.ppermute(value, 'space', pairs)  11 us
    pallas_call x1, Pallas kernels, sums_along_z(): pl.pallas_call(functools.partial(sums_kernel, layers, groups), out_shape=...  10.9 us
    unnamed x39, local copies, waits for them, and re-layouts  10.6 us
    pallas_call x1, Pallas kernels, partial_sums(): pl.pallas_call(partial_kernel, out_shape=[jax.ShapeDtypeStruct(s, F32) fo...  7.98 us
    all_to_all x1, starting transfers between devices, body(): lax.all_to_all(spread_out.reshape(COUNT, 16, SIDE), 'space', 0, 0, tiled=...  7.93 us
  transfers between devices with their start and end apart: 8, of which 3 were waited for; matrix products, arithmetic and copies ran while one was open for 1% of the time, Pallas kernels for 22%

profile of v1, /device:TPU:2, one launch (start us, length us, event | category | flops | bytes accessed | tf_op | source)
XLA Modules:
  0.0 122.4 jit_solution(16435850008363666016)
XLA Ops:
  0.0 0.9 copy-done.10
  1.0 0.8 copy-done.12
  1.8 8.0 %partial.1 = (f32[2,128,128]{2,1,0:T(8,128)}, f32[2,128,128]{2,1,0:T(8,128)}, f32[9,128,128]{2,1,0:T(8,128)S(1)}, f32[32,16,128]{2,1,0:T(8,128)}) custom-call(f32[4,16,128,128]{3,2,1,0:T(8,128)} %v_high.3, bf16[512,256]{1,0:T(8,128)(2,1)S(1)} %copy-done.10, f32[96,128]{1,0:T(8,128)S(1)} %copy-done.12), custom_call_target="tpu_custom_call" | custom-call | flops 1000 | bytes 1000 | tf_op jit(solution)/shard_map/partial/pallas_call | solution.py:277
  9.7 0.0 copy-start.4
  9.8 0.8 copy-done.4
  10.6 11.5 %all-to-all-start = ((f32[32,16,128]{2,1,0:T(8,128)}), f32[32,16,128]{2,1,0:T(8,128)S(1)}, u32[]{:S(2)}, u32[]{:S(2)}) async-start(f32[32,16,128]{2,1,0:T(8,128)} %get-tuple-element.21), calls=%async_computation | async-start | bytes 524288 | tf_op jit(solution)/shard_map/all_to_all | solution.py:660
  22.1 1.9 %collective-permute-start = (f32[2,128,128]{2,1,0:T(8,128)}, f32[2,128,128]{2,1,0:T(8,128)S(1)}, u32[]{:S(2)}, u32[]{:S(2)}) collective-permute-start(f32[2,128,128]{2,1,0:T(8,128)} %get-tuple-element.19), channel_id=1, source_target_pairs={{0,1},{1,2},{2,3},{3,4},{4,5},{5,6},{6,7},{7,8},{8,9},{9,10},{10,1... | collective-permute-start | bytes 393224 | tf_op jit(solution)/shard_map/ppermute | solution.py:568
  23.9 3.6 %collective-permute-start.1 = (f32[2,128,128]{2,1,0:T(8,128)}, f32[2,128,128]{2,1,0:T(8,128)S(1)}, u32[]{:S(2)}, u32[]{:S(2)}) collective-permute-start(f32[2,128,128]{2,1,0:T(8,128)} %get-tuple-element.20), channel_id=1, source_target_pairs={{0,31},{1,0},{2,1},{3,2},{4,3},{5,4},{6,5},{7,6},{8,7},{9,8},{10,9... | collective-permute-start | bytes 393224 | tf_op jit(solution)/shard_map/ppermute | solution.py:568
  27.5 0.0 copy-done.18
  27.5 0.1 reshape_reshape_squeeze.3.taps_ref
  27.6 0.1 copy.13
  27.7 0.0 copy-done.17
  27.7 0.3 convolution_bitcast_fusion.rows_ref
  28.0 0.0 copy-done.16
  28.0 0.6 fusion.cols_ref
  28.6 2.9 %modes.1 = (f32[15,256,128]{2,1,0:T(8,128)S(1)}, f32[15,128,128]{2,1,0:T(8,128)S(1)}, f32[80,128]{1,0:T(8,128)S(1)}) custom-call(s32[1]{0:T(128)} %bitcast.1.me_ref, f32[240]{0:T(256)S(1)} %reshape_reshape_squeeze.3.taps_ref, f32[48,1024]{1,0:T(8,128)S(1)} %convolution_bitcast_fusion.rows_ref, f32[1024,48]{1,0:T(8,128)S(1)} %fusion.cols_ref, ...), custom_call_target="tpu_custom_call" | custom-call | flops 1000 | bytes 1000 | tf_op jit(solution)/shard_map/modes/pallas_call | solution.py:642
  31.5 1.0 copy-done.6
  32.5 0.6 copy-done.14
  33.1 2.8 %all-to-all-done = f32[32,16,128]{2,1,0:T(8,128)S(1)} async-done(((f32[32,16,128]{2,1,0:T(8,128)}), f32[32,16,128]{2,1,0:T(8,128)S(1)}, u32[]{:S(2)}, u32[]{:S(2)}) %all-to-all-start) | async-done | bytes 262176 | tf_op jit(solution)/shard_map/all_to_all | solution.py:660
  35.9 0.8 copy-done.15
  36.7 1.9 %along.1.token = f32[512,128]{1,0:T(8,128)} custom-call(f32[512,128]{1,0:T(8,128)S(1)} %bitcast.16, f32[80,128]{1,0:T(8,128)S(1)} %copy-done.15), custom_call_target="tpu_custom_call" | custom-call | flops 99999997952 | bytes 400000000 | tf_op jit(solution)/shard_map/along/pallas_call | solution.py:346
  38.6 0.0 collective-permute-done.from_below
  38.6 0.0 collective-permute-done.1.from_above
  38.6 0.0 copy-done.1
  38.6 0.0 copy-done.5
  38.6 5.9 %near.1 = (f32[5,2,2,128,128]{4,3,2,1,0:T(8,128)}, f32[5,2,2,128,128]{4,3,2,1,0:T(8,128)}) custom-call(f32[4,16,128,128]{3,2,1,0:T(8,128)} %v_high.3, f32[4,16,128,128]{3,2,1,0:T(8,128)} %v_high.3, bf16[8,256,256]{2,1,0:T(8,128)(2,1)S(1)} %copy-done.1, f32[9,128,128]{2,1,0:T(8,128)S(1)} %copy-done.5, f32[2,128,128]{2,1,0:T(8,128)S(1)} %collective-permute-done.from_below, ...), custom_call_target="tpu_custom_call" | custom-call | flops 1000 | bytes 1000 | tf_op jit(solution)/shard_map/near/pallas_call | solution.py:138
  44.5 0.0 collective-permute-start.3
  44.5 2.0 %collective-permute-start.2 = (f32[5,2,2,128,128]{4,3,2,1,0:T(8,128)}, f32[5,2,2,128,128]{4,3,2,1,0:T(8,128)}, u32[]{:S(2)}, u32[]{:S(2)}) collective-permute-start(f32[5,2,2,128,128]{4,3,2,1,0:T(8,128)} %get-tuple-element.28.refs_5_.own), channel_id=1, source_target_pairs={{0,1},{1,2},{2,3},{3,4},{4,5},{5,6},{6,7},{7,8},{8,9},{9,10},{10,1... | collective-permute-start | bytes 3932168 | tf_op jit(solution)/shard_map/ppermute | solution.py:568
  46.5 7.0 %far.1 = (f32[4,2,2,128,128]{4,3,2,1,0:T(8,128)}, f32[4,2,2,128,128]{4,3,2,1,0:T(8,128)}, f32[1,2,2,128,128]{4,3,2,1,0:T(8,128)S(1)}, f32[1,2,2,128,128]{4,3,2,1,0:T(8,128)S(1)}) custom-call(f32[4,16,128,128]{3,2,1,0:T(8,128)} %v_high.3, f32[4,16,128,128]{3,2,1,0:T(8,128)} %v_high.3, bf16[8,256,256]{2,1,0:T(8,128)(2,1)S(1)} %copy-done.1, ...), custom_call_target="tpu_custom_call" | custom-call | flops 1000 | bytes 1000 | tf_op jit(solution)/shard_map/far/pallas_call | solution.py:177
  53.6 0.7 copy-done.8
  54.3 3.5 %collective-permute-start.5 = (f32[4,2,2,128,128]{4,3,2,1,0:T(8,128)}, f32[4,2,2,128,128]{4,3,2,1,0:T(8,128)}, u32[]{:S(2)}, u32[]{:S(2)}) collective-permute-start(f32[4,2,2,128,128]{4,3,2,1,0:T(8,128)} %get-tuple-element.24.refs_1_), channel_id=1, source_target_pairs={{0,31},{1,0},{2,1},{3,2},{4,3},{5,4},{6,5},{7,6},{8,7},{9,8},{10,9... | collective-permute-start | bytes 3145736 | tf_op jit(solution)/shard_map/ppermute | solution.py:568
  57.8 0.0 collective-permute-start.4
  57.8 7.9 %all-to-all-start.1 = ((f32[32,16,128]{2,1,0:T(8,128)}), f32[32,16,128]{2,1,0:T(8,128)S(1)}, u32[]{:S(2)}, u32[]{:S(2)}) async-start(f32[32,16,128]{2,1,0:T(8,128)} %bitcast.6), calls=%async_computation.1 | async-start | bytes 524288 | tf_op jit(solution)/shard_map/all_to_all | solution.py:669
  65.7 0.9 copy-done.9
  66.7 10.9 %sums.1.acc = f32[16,2,2,128,128]{4,3,2,1,0:T(8,128)S(1)} custom-call(f32[5,2,2,128,128]{4,3,2,1,0:T(8,128)} %get-tuple-element.23.refs_0_.last, f32[4,2,2,128,128]{4,3,2,1,0:T(8,128)} %get-tuple-element.24.refs_1_, f32[1,2,2,128,128]{4,3,2,1,0:T(8,128)S(1)} %get-tuple-element.25.refs_2_, f32[1,2,2,128,128]{4,3,2,1,0:T(8,128)S(1)} %copy-done.9, ...), custom_call_target="tpu_custom_call" | custom-call | flops 1000 | bytes 1000 | tf_op jit(solution)/shard_map/sums/pallas_call | solution.py:438
  77.6 0.0 copy-start
  77.6 2.0 %copy-done = f32[16,2,2,128,128]{4,3,2,1,0:T(8,128)} copy-done((f32[16,2,2,128,128]{4,3,2,1,0:T(8,128)}, f32[16,2,2,128,128]{4,3,2,1,0:T(8,128)S(1)}, u32[]{:S(2)}) %copy-start) | copy-done | bytes 4194328
  79.6 0.0 collective-permute-done.3.above.near_high
  79.6 2.3 %collective-permute-done.2.below.near_low = f32[5,2,2,128,128]{4,3,2,1,0:T(8,128)} collective-permute-done((f32[5,2,2,128,128]{4,3,2,1,0:T(8,128)}, f32[5,2,2,128,128]{4,3,2,1,0:T(8,128)}, u32[]{:S(2)}, u32[]{:S(2)}) %collective-permute-start.2) | collective-permute-done | bytes 1310752 | tf_op jit(solution)/shard_map/ppermute | solution.py:568
  81.9 0.0 copy-done.7
  81.9 4.5 %level.1 = f32[11,128,128]{2,1,0:T(8,128)S(1)} custom-call(f32[5,2,2,128,128]{4,3,2,1,0:T(8,128)} %collective-permute-done.2.below.near_low, f32[5,2,2,128,128]{4,3,2,1,0:T(8,128)} %get-tuple-element.28.refs_5_.own, f32[5,2,2,128,128]{4,3,2,1,0:T(8,128)} %get-tuple-element.23.refs_0_.last, f32[5,2,2,128,128]{4,3,2,1,0:T(8,128)} %collective-permute-done.3.above.near_high, ...), custom_call_target="tpu_custom_call" | custom-call | flops 1000 | bytes 1000 | tf_op jit(solution)/shard_map/level/pallas_call | solution.py:379
  86.4 0.0 copy-start.2
  86.4 0.8 copy-done.2
  87.3 19.5 %all-to-all-done.1.y_ref = f32[32,16,128]{2,1,0:T(8,128)S(1)} async-done(((f32[32,16,128]{2,1,0:T(8,128)}), f32[32,16,128]{2,1,0:T(8,128)S(1)}, u32[]{:S(2)}, u32[]{:S(2)}) %all-to-all-start.1) | async-done | bytes 262176 | tf_op jit(solution)/shard_map/all_to_all | solution.py:669
  106.8 0.0 collective-permute-done.5.far_high
  106.8 0.0 collective-permute-done.4.far_low
  106.8 1.1 copy-done.3
  107.9 14.4 %finish.1 = f32[4,16,128,128]{3,2,1,0:T(8,128)} custom-call(f32[16,2,2,128,128]{4,3,2,1,0:T(8,128)} %copy-done, f32[5,2,2,128,128]{4,3,2,1,0:T(8,128)} %collective-permute-done.2.below.near_low, f32[5,2,2,128,128]{4,3,2,1,0:T(8,128)} %collective-permute-done.3.above.near_high, f32[4,2,2,128,128]{4,3,2,1,0:T(8,128)} %collective-permute-done.4.far_low, ...), custom_call_target="tpu_custom_call" | custom-call | flops 1000 | bytes 1000 | tf_op jit(solution)/shard_map/finish/pallas_call | solution.py:518
  (21 shorter events, 0.1 us)
Async XLA Ops:
  0.0 0.9 copy-start.10
  1.0 0.8 copy-start.12
  1.8 25.7 %copy-start.18 = (f32[4,4,3,15]{3,1,2,0:T(4,128)S(1)}, f32[4,4,3,15]{3,1,2,0:T(4,128)}, u32[]{:S(2)}) copy-start(f32[4,4,3,15]{3,1,2,0:T(4,128)} %param.10) | copy-start | bytes 8644
  1.8 25.9 %copy-start.17 = (f32[15,1024]{1,0:T(8,128)S(1)}, f32[15,1024]{1,0:T(8,128)}, u32[]{:S(2)}) copy-start(f32[15,1024]{1,0:T(8,128)} %constant.21.clone) | copy-start | bytes 184324
  1.8 26.3 %copy-start.16 = (f32[1024,15]{1,0:T(8,128)S(1)}, f32[1024,15]{1,0:T(8,128)}, u32[]{:S(2)}) copy-start(f32[1024,15]{1,0:T(8,128)} %constant.22.clone) | copy-start | bytes 184324
  9.7 0.8 copy-start.4
  10.6 25.4 %all-to-all-start = ((f32[32,16,128]{2,1,0:T(8,128)}), f32[32,16,128]{2,1,0:T(8,128)S(1)}, u32[]{:S(2)}, u32[]{:S(2)}) async-start(f32[32,16,128]{2,1,0:T(8,128)} %get-tuple-element.21), calls=%async_computation | async-start | bytes 524288 | tf_op jit(solution)/shard_map/all_to_all | solution.py:660
  22.1 16.6 %collective-permute-start = (f32[2,128,128]{2,1,0:T(8,128)}, f32[2,128,128]{2,1,0:T(8,128)S(1)}, u32[]{:S(2)}, u32[]{:S(2)}) collective-permute-start(f32[2,128,128]{2,1,0:T(8,128)} %get-tuple-element.19), channel_id=1, source_target_pairs={{0,1},{1,2},{2,3},{3,4},{4,5},{5,6},{6,7},{7,8},{8,9},{9,10},{10,1... | collective-permute-start | bytes 393224 | tf_op jit(solution)/shard_map/ppermute | solution.py:568
  23.9 14.7 %collective-permute-start.1 = (f32[2,128,128]{2,1,0:T(8,128)}, f32[2,128,128]{2,1,0:T(8,128)S(1)}, u32[]{:S(2)}, u32[]{:S(2)}) collective-permute-start(f32[2,128,128]{2,1,0:T(8,128)} %get-tuple-element.20), channel_id=1, source_target_pairs={{0,31},{1,0},{2,1},{3,2},{4,3},{5,4},{6,5},{7,6},{8,7},{9,8},{10,9... | collective-permute-start | bytes 393224 | tf_op jit(solution)/shard_map/ppermute | solution.py:568
  31.5 1.1 copy-start.6
  32.5 0.6 copy-start.14
  35.9 0.8 copy-start.15
  36.7 1.9 %copy-start.1 = (bf16[8,256,256]{2,1,0:T(8,128)(2,1)S(1)}, bf16[8,256,256]{2,1,0:T(8,128)(2,1)}, u32[]{:S(2)}) copy-start(bf16[8,256,256]{2,1,0:T(8,128)(2,1)} %constant.18.clone.mats) | copy-start | bytes 3145732
  36.7 1.9 %copy-start.5 = (f32[9,128,128]{2,1,0:T(8,128)S(1)}, f32[9,128,128]{2,1,0:T(8,128)}, u32[]{:S(2)}) copy-start(f32[9,128,128]{2,1,0:T(8,128)} %copy-done.4) | copy-start | bytes 1769476
  44.5 35.1 %collective-permute-start.3 = (f32[5,2,2,128,128]{4,3,2,1,0:T(8,128)}, f32[5,2,2,128,128]{4,3,2,1,0:T(8,128)}, u32[]{:S(2)}, u32[]{:S(2)}) collective-permute-start(f32[5,2,2,128,128]{4,3,2,1,0:T(8,128)} %get-tuple-element.23.refs_0_.last), channel_id=1, source_target_pairs={{0,31},{1,0},{2,1},{3,2},{4,3},{5,4},{6,5},{7,6},{8,7},{9,8},{10,9... | collective-permute-start | bytes 3932168 | tf_op jit(solution)/shard_map/ppermute | solution.py:568
  44.5 37.4 %collective-permute-start.2 = (f32[5,2,2,128,128]{4,3,2,1,0:T(8,128)}, f32[5,2,2,128,128]{4,3,2,1,0:T(8,128)}, u32[]{:S(2)}, u32[]{:S(2)}) collective-permute-start(f32[5,2,2,128,128]{4,3,2,1,0:T(8,128)} %get-tuple-element.28.refs_5_.own), channel_id=1, source_target_pairs={{0,1},{1,2},{2,3},{3,4},{4,5},{5,6},{6,7},{7,8},{8,9},{9,10},{10,1... | collective-permute-start | bytes 3932168 | tf_op jit(solution)/shard_map/ppermute | solution.py:568
  53.6 0.7 copy-start.8
  54.3 52.5 %collective-permute-start.5 = (f32[4,2,2,128,128]{4,3,2,1,0:T(8,128)}, f32[4,2,2,128,128]{4,3,2,1,0:T(8,128)}, u32[]{:S(2)}, u32[]{:S(2)}) collective-permute-start(f32[4,2,2,128,128]{4,3,2,1,0:T(8,128)} %get-tuple-element.24.refs_1_), channel_id=1, source_target_pairs={{0,31},{1,0},{2,1},{3,2},{4,3},{5,4},{6,5},{7,6},{8,7},{9,8},{10,9... | collective-permute-start | bytes 3145736 | tf_op jit(solution)/shard_map/ppermute | solution.py:568
  57.8 49.0 %collective-permute-start.4 = (f32[4,2,2,128,128]{4,3,2,1,0:T(8,128)}, f32[4,2,2,128,128]{4,3,2,1,0:T(8,128)}, u32[]{:S(2)}, u32[]{:S(2)}) collective-permute-start(f32[4,2,2,128,128]{4,3,2,1,0:T(8,128)} %get-tuple-element.27.refs_4_), channel_id=1, source_target_pairs={{0,1},{1,2},{2,3},{3,4},{4,5},{5,6},{6,7},{7,8},{8,9},{9,10},{10,1... | collective-permute-start | bytes 3145736 | tf_op jit(solution)/shard_map/ppermute | solution.py:568
  57.8 49.0 %all-to-all-start.1 = ((f32[32,16,128]{2,1,0:T(8,128)}), f32[32,16,128]{2,1,0:T(8,128)S(1)}, u32[]{:S(2)}, u32[]{:S(2)}) async-start(f32[32,16,128]{2,1,0:T(8,128)} %bitcast.6), calls=%async_computation.1 | async-start | bytes 524288 | tf_op jit(solution)/shard_map/all_to_all | solution.py:669
  65.7 1.0 copy-start.9
  66.7 15.2 %copy-start.7 = (f32[15,128,128]{2,1,0:T(8,128)S(1)}, f32[15,128,128]{2,1,0:T(8,128)}, u32[]{:S(2)}) copy-start(f32[15,128,128]{2,1,0:T(8,128)} %copy-done.6) | copy-start | bytes 2949124
  77.6 2.0 %copy-start = (f32[16,2,2,128,128]{4,3,2,1,0:T(8,128)}, f32[16,2,2,128,128]{4,3,2,1,0:T(8,128)S(1)}, u32[]{:S(2)}) copy-start(f32[16,2,2,128,128]{4,3,2,1,0:T(8,128)S(1)} %sums.1.acc) | copy-start | bytes 12582916
  81.9 24.9 %copy-start.11 = (f32[128,128]{1,0:T(8,128)S(1)}, f32[128,128]{1,0:T(8,128)}, u32[]{:S(2)}) copy-start(f32[128,128]{1,0:T(8,128)} %constant.24.clone.spread) | copy-start | bytes 196612
  81.9 24.9 %copy-start.13 = (f32[64,128]{1,0:T(8,128)S(1)}, f32[64,128]{1,0:T(8,128)}, u32[]{:S(2)}) copy-start(f32[64,128]{1,0:T(8,128)} %constant.23.clone.small) | copy-start | bytes 98308
  86.4 0.9 copy-start.2
  106.8 1.1 copy-start.3

commit v2 on v1

--- a/solution.py
+++ b/solution.py
@@ -413,7 +413,9 @@
         out_ref[z] = total
 
 
-def sums_kernel(layers, groups, *refs):
+def sums_kernel(layers, groups, added, *refs):
+    start = refs[0]
+    refs = refs[1:] if added else refs
     sources, w_ref, out = refs[:-2], refs[-2], refs[-1]
     for k, z in enumerate(groups):
         def block(r, carry):
@@ -428,24 +430,28 @@
             sums = slide(4, 2, value, lambda t: (w_ref[t, 0, rows], w_ref[t, 1, rows]))
             for i in range(4):
                 for n in range(4):
-                    out[4 * k + i, n // 2, n % 2, rows] = sums[i][n]
+                    total = sums[i][n]
+                    if added:
+                        before = start[4 * k + i, n // 2, n % 2, rows]
+                        total = before if total is None else before + total
+                    out[4 * k + i, n // 2, n % 2, rows] = total
             return carry
 
         lax.fori_loop(0, SIDE // 8, block, 0)
 
 
-def sums_along_z(pieces, layers, groups, w0):
+def sums_along_z(pieces, layers, groups, w0, start=None):
     return pl.pallas_call(
-        functools.partial(sums_kernel, layers, groups),
+        functools.partial(sums_kernel, layers, groups, start is not None),
         out_shape=jax.ShapeDtypeStruct((4 * len(groups), 2, 2, SIDE, SIDE), F32),
         compiler_params=params(24),
         name="sums",
         cost_estimate=pl.CostEstimate(flops=1000, bytes_accessed=1000, transcendentals=0),
-    )(*pieces, w0)
+    )(*(() if start is None else (start,)), *pieces, w0)
 
 
 def finish_kernel(
-    acc, near_low, near_high, far_low, far_high, w_ref, level, y_ref, small, spread, mats, out, coarse, p_ref, sum_ref
+    acc, far_low, far_high, w_ref, level, y_ref, small, spread, mats, out, coarse, p_ref, sum_ref
 ):
     step = pl.program_id(0)
 
@@ -453,8 +459,7 @@
     def _():
         spread_levels(level, y_ref, small, coarse, p_ref)
 
-    halo = [(far_low, k, k - 7) for k in range(4)] + [(near_low, k, k - 3) for k in range(3)]
-    halo += [(near_high, k, 16 + k) for k in range(3)] + [(far_high, k, 19 + k) for k in range(4)]
+    halo = [(far_low, k, k - 7) for k in range(4)] + [(far_high, k, 19 + k) for k in range(4)]
 
     def add_halo(first):
         def block(r, carry):
@@ -476,7 +481,7 @@
 
         lax.fori_loop(0, SIDE // 8, block, 0)
 
-    for number, first in enumerate((4, 6, 8, 10, 0, 2, 12, 14)):
+    for number, first in ((4, 0), (5, 2), (6, 12), (7, 14)):
         @pl.when(step == number)
         def _():
             add_halo(first)
@@ -484,29 +489,38 @@
     lane = lax.broadcasted_iota(jnp.int32, (64, SIDE), 1)
     z = 2 * pair_of_layers(step)
 
-    columns = []
-    for i in range(2):
-        sides = [[], []]
-        for part in range(2):
-            g = coarse[z + i, 64 * part : 64 * part + 64]
-            h = pltpu.roll(g, 64, 1)
-            for pair in range(2):
-                tile = jnp.where((lane < 64) == (pair == 0), g, h)
-                for row in (0, 64):
-                    sides[pair].append(sum_ref[i, pair, part, row : row + 64] + spread[row : row + 64] * tile)
-        columns += [jnp.concatenate(side, 0) for side in sides]
-    c = left_mul(mats[0], mats[1], jnp.concatenate(columns, 1))
-    rows = jnp.concatenate(
-        [
-            jnp.concatenate([c[:SIDE, SIDE * n : SIDE * n + SIDE], c[SIDE:, SIDE * n : SIDE * n + SIDE]], 1)
-            for n in range(4)
-        ],
-        0,
-    )
-    d = right_mul(rows, mats[2], mats[3])
-    for n in range(4):
-        for half in range(2):
-            out[2 * (n % 2) + half, n // 2] = d[SIDE * n : SIDE * n + SIDE, SIDE * half : SIDE * half + SIDE]
+    def run(modes):
+        columns = []
+        for i in range(2):
+            sides = [[], []]
+            for part in range(2):
+                g = coarse[z + i, 64 * part : 64 * part + 64]
+                h = pltpu.roll(g, 64, 1)
+                for pair in range(2):
+                    tile = jnp.where((lane < 64) == (pair == 0), g, h)
+                    for row in (0, 64):
+                        sides[pair].append(modes[i, pair, part, row : row + 64] + spread[row : row + 64] * tile)
+            columns += [jnp.concatenate(side, 0) for side in sides]
+        c = left_mul(mats[0], mats[1], jnp.concatenate(columns, 1))
+        rows = jnp.concatenate(
+            [
+                jnp.concatenate([c[:SIDE, SIDE * n : SIDE * n + SIDE], c[SIDE:, SIDE * n : SIDE * n + SIDE]], 1)
+                for n in range(4)
+            ],
+            0,
+        )
+        d = right_mul(rows, mats[2], mats[3])
+        for n in range(4):
+            for half in range(2):
+                out[2 * (n % 2) + half, n // 2] = d[SIDE * n : SIDE * n + SIDE, SIDE * half : SIDE * half + SIDE]
+
+    @pl.when(step < 4)
+    def _():
+        run(acc)
+
+    @pl.when(step >= 4)
+    def _():
+        run(sum_ref)
 
 
 def pair_of_layers(step):
@@ -515,13 +529,12 @@
 
 def finish(acc, halos, w0, level, potentials, mats):
     full, half = spread_weights()
+    tables = [pltpu.with_memory_space_constraint(jnp.asarray(t), pltpu.HBM) for t in (half, full)]
     return pl.pallas_call(
         finish_kernel,
         grid=(8,),
         in_specs=[
             pl.BlockSpec((2, 2, 2, SIDE, SIDE), lambda i: (pair_of_layers(i), 0, 0, 0, 0)),
-            whole((5, 2, 2, SIDE, SIDE)),
-            whole((5, 2, 2, SIDE, SIDE)),
             whole((4, 2, 2, SIDE, SIDE)),
             whole((4, 2, 2, SIDE, SIDE)),
             whole((TAPS, 2, SIDE, SIDE)),
@@ -541,7 +554,7 @@
         compiler_params=params(28),
         name="finish",
         cost_estimate=pl.CostEstimate(flops=1000, bytes_accessed=1000, transcendentals=0),
-    )(acc, *halos, w0, level, potentials, jnp.asarray(half), jnp.asarray(full), mats)
+    )(acc, *halos, w0, level, potentials, *tables, mats)
 
 
 def slide(outputs, pairs, value, weight):
@@ -675,9 +688,12 @@
     places = ((0, 3), (3, 4), (7, 1), (8, 1), (9, 4), (13, 3))
     layers = {first + i: (k, i) for k, (first, count) in enumerate(places) for i in range(count)}
     acc = sums_along_z(pieces, layers, (0, 4, 8, 12), w0)
+    halo = {z: (k, i) for k, first in enumerate((-3, 16)) for i, z in enumerate(range(first, first + 3))}
+    acc = sums_along_z((near_lower, near_upper), halo, (0, 4, 8, 12), w0, acc)
     acc = pltpu.with_memory_space_constraint(acc, pltpu.HBM)
     level = level_one(near_lower, near_up, near_down, near_upper, w1)
-    return finish(acc, (near_lower, near_upper, far_lower, far_upper), w0, level, potentials, mats)
+    level = pltpu.with_memory_space_constraint(level, pltpu.HBM)
+    return finish(acc, (far_lower, far_upper), w0, level, potentials, mats)
 
 
 def solution(mesh):

time: 123 us -> 120 us (0.976)
  waiting for transfers between devices: 24.7 us -> 21.1 us
  Pallas kernels: 55.5 us -> 56.8 us
    all_to_all x1, waiting for transfers between devices: 19.5 us -> 13.9 us  [body(): lax.all_to_all(spread_out.reshape(COUNT, 16, SIDE), 'space', 0, 0, tiled=...]
    pallas_call x1 -> x2, Pallas kernels: 10.9 us -> 14.5 us  [sums_along_z(): pl.pallas_call(functools.partial(sums_kernel, layers, groups, start is no...]
    pallas_call x1, Pallas kernels: 14.4 us -> 12.2 us  [finish(): pl.pallas_call(finish_kernel, grid=(8,), in_specs=[pl.BlockSpec((2, 2, 2,...]
    ppermute x6, waiting for transfers between devices: 2.36 us -> 4.35 us  [shifted(): return lax.ppermute(value, 'space', pairs)]
    unnamed x39 -> x33, local copies, waits for them, and re-layouts: 10.6 us -> 9.55 us
  transfers between devices with their start and end apart: 8 -> 8, of which waited for: 3 -> 4; matrix products, arithmetic and copies ran while one was open for 1% -> 1% of each run, Pallas kernels for 22% -> 26%
where the time goes in v2:
time: 120 us; the launch traced here: 119 us
  Pallas kernels  56.8 us (47%)
  starting transfers between devices  30.4 us (25%)
  waiting for transfers between devices  21.1 us (18%)
  local copies, waits for them, and re-layouts  9.74 us (8%)
    pallas_call x2, Pallas kernels, sums_along_z(): pl.pallas_call(functools.partial(sums_kernel, layers, groups, start is no...  14.5 us
    all_to_all x1, waiting for transfers between devices, body(): lax.all_to_all(spread_out.reshape(COUNT, 16, SIDE), 'space', 0, 0, tiled=...  13.9 us
    pallas_call x1, Pallas kernels, finish(): pl.pallas_call(finish_kernel, grid=(8,), in_specs=[pl.BlockSpec((2, 2, 2,...  12.2 us
    all_to_all x1, starting transfers between devices, body(): received = lax.all_to_all(payload, 'space', 0, 0, tiled=True)  11.5 us
    ppermute x6, starting transfers between devices, shifted(): return lax.ppermute(value, 'space', pairs)  11 us
    unnamed x33, local copies, waits for them, and re-layouts  9.55 us
    pallas_call x1, Pallas kernels, partial_sums(): pl.pallas_call(partial_kernel, out_shape=[jax.ShapeDtypeStruct(s, F32) fo...  7.98 us
    all_to_all x1, starting transfers between devices, body(): lax.all_to_all(spread_out.reshape(COUNT, 16, SIDE), 'space', 0, 0, tiled=...  7.9 us
  transfers between devices with their start and end apart: 8, of which 4 were waited for; matrix products, arithmetic and copies ran while one was open for 1% of the time, Pallas kernels for 26%

profile of v2, /device:TPU:2, one launch (start us, length us, event | category | flops | bytes accessed | tf_op | source)
XLA Modules:
  0.0 119.0 jit_solution(16564947339489638129)
XLA Ops:
  0.0 0.9 copy-done.9
  1.0 0.8 copy-done.10
  1.8 8.0 %partial.1 = (f32[2,128,128]{2,1,0:T(8,128)}, f32[2,128,128]{2,1,0:T(8,128)}, f32[9,128,128]{2,1,0:T(8,128)S(1)}, f32[32,16,128]{2,1,0:T(8,128)}) custom-call(f32[4,16,128,128]{3,2,1,0:T(8,128)} %v_high.3, bf16[512,256]{1,0:T(8,128)(2,1)S(1)} %copy-done.9, f32[96,128]{1,0:T(8,128)S(1)} %copy-done.10), custom_call_target="tpu_custom_call" | custom-call | flops 1000 | bytes 1000 | tf_op jit(solution)/shard_map/partial/pallas_call | solution.py:277
  9.7 0.0 copy-start.3
  9.8 0.8 copy-done.3
  10.6 11.5 %all-to-all-start = ((f32[32,16,128]{2,1,0:T(8,128)}), f32[32,16,128]{2,1,0:T(8,128)S(1)}, u32[]{:S(2)}, u32[]{:S(2)}) async-start(f32[32,16,128]{2,1,0:T(8,128)} %get-tuple-element.21), calls=%async_computation | async-start | bytes 524288 | tf_op jit(solution)/shard_map/all_to_all | solution.py:673
  22.1 1.9 %collective-permute-start = (f32[2,128,128]{2,1,0:T(8,128)}, f32[2,128,128]{2,1,0:T(8,128)S(1)}, u32[]{:S(2)}, u32[]{:S(2)}) collective-permute-start(f32[2,128,128]{2,1,0:T(8,128)} %get-tuple-element.19), channel_id=1, source_target_pairs={{0,1},{1,2},{2,3},{3,4},{4,5},{5,6},{6,7},{7,8},{8,9},{9,10},{10,1... | collective-permute-start | bytes 393224 | tf_op jit(solution)/shard_map/ppermute | solution.py:581
  23.9 3.6 %collective-permute-start.1 = (f32[2,128,128]{2,1,0:T(8,128)}, f32[2,128,128]{2,1,0:T(8,128)S(1)}, u32[]{:S(2)}, u32[]{:S(2)}) collective-permute-start(f32[2,128,128]{2,1,0:T(8,128)} %get-tuple-element.20), channel_id=1, source_target_pairs={{0,31},{1,0},{2,1},{3,2},{4,3},{5,4},{6,5},{7,6},{8,7},{9,8},{10,9... | collective-permute-start | bytes 393224 | tf_op jit(solution)/shard_map/ppermute | solution.py:581
  27.5 0.0 copy-done.15
  27.5 0.1 reshape_reshape_squeeze.3.taps_ref
  27.6 0.1 copy.13
  27.7 0.0 copy-done.14
  27.7 0.3 convolution_bitcast_fusion.rows_ref
  28.0 0.0 copy-done.13
  28.0 0.6 fusion.cols_ref
  28.6 2.9 %modes.1 = (f32[15,256,128]{2,1,0:T(8,128)S(1)}, f32[15,128,128]{2,1,0:T(8,128)S(1)}, f32[80,128]{1,0:T(8,128)S(1)}) custom-call(s32[1]{0:T(128)} %bitcast.1.me_ref, f32[240]{0:T(256)S(1)} %reshape_reshape_squeeze.3.taps_ref, f32[48,1024]{1,0:T(8,128)S(1)} %convolution_bitcast_fusion.rows_ref, f32[1024,48]{1,0:T(8,128)S(1)} %fusion.cols_ref, ...), custom_call_target="tpu_custom_call" | custom-call | flops 1000 | bytes 1000 | tf_op jit(solution)/shard_map/modes/pallas_call | solution.py:655
  31.5 1.1 copy-done.5
  32.5 0.6 copy-done.11
  33.1 2.8 %all-to-all-done = f32[32,16,128]{2,1,0:T(8,128)S(1)} async-done(((f32[32,16,128]{2,1,0:T(8,128)}), f32[32,16,128]{2,1,0:T(8,128)S(1)}, u32[]{:S(2)}, u32[]{:S(2)}) %all-to-all-start) | async-done | bytes 262176 | tf_op jit(solution)/shard_map/all_to_all | solution.py:673
  35.9 0.8 copy-done.12
  36.7 1.9 %along.1.token = f32[512,128]{1,0:T(8,128)} custom-call(f32[512,128]{1,0:T(8,128)S(1)} %bitcast.17, f32[80,128]{1,0:T(8,128)S(1)} %copy-done.12), custom_call_target="tpu_custom_call" | custom-call | flops 99999997952 | bytes 400000000 | tf_op jit(solution)/shard_map/along/pallas_call | solution.py:346
  38.6 0.0 collective-permute-done.from_below
  38.6 0.0 collective-permute-done.1.from_above
  38.6 0.0 copy-done.1
  38.6 0.0 copy-done.4
  38.7 5.8 %near.1 = (f32[5,2,2,128,128]{4,3,2,1,0:T(8,128)}, f32[5,2,2,128,128]{4,3,2,1,0:T(8,128)}) custom-call(f32[4,16,128,128]{3,2,1,0:T(8,128)} %v_high.3, f32[4,16,128,128]{3,2,1,0:T(8,128)} %v_high.3, bf16[8,256,256]{2,1,0:T(8,128)(2,1)S(1)} %copy-done.1, f32[9,128,128]{2,1,0:T(8,128)S(1)} %copy-done.4, f32[2,128,128]{2,1,0:T(8,128)S(1)} %collective-permute-done.from_below, ...), custom_call_target="tpu_custom_call" | custom-call | flops 1000 | bytes 1000 | tf_op jit(solution)/shard_map/near/pallas_call | solution.py:138
  44.5 0.0 collective-permute-start.3
  44.5 2.0 %collective-permute-start.2 = (f32[5,2,2,128,128]{4,3,2,1,0:T(8,128)}, f32[5,2,2,128,128]{4,3,2,1,0:T(8,128)}, u32[]{:S(2)}, u32[]{:S(2)}) collective-permute-start(f32[5,2,2,128,128]{4,3,2,1,0:T(8,128)} %get-tuple-element.28.refs_5_.own), channel_id=1, source_target_pairs={{0,1},{1,2},{2,3},{3,4},{4,5},{5,6},{6,7},{7,8},{8,9},{9,10},{10,1... | collective-permute-start | bytes 3932168 | tf_op jit(solution)/shard_map/ppermute | solution.py:581
  46.5 7.0 %far.1 = (f32[4,2,2,128,128]{4,3,2,1,0:T(8,128)}, f32[4,2,2,128,128]{4,3,2,1,0:T(8,128)}, f32[1,2,2,128,128]{4,3,2,1,0:T(8,128)S(1)}, f32[1,2,2,128,128]{4,3,2,1,0:T(8,128)S(1)}) custom-call(f32[4,16,128,128]{3,2,1,0:T(8,128)} %v_high.3, f32[4,16,128,128]{3,2,1,0:T(8,128)} %v_high.3, bf16[8,256,256]{2,1,0:T(8,128)(2,1)S(1)} %copy-done.1, ...), custom_call_target="tpu_custom_call" | custom-call | flops 1000 | bytes 1000 | tf_op jit(solution)/shard_map/far/pallas_call | solution.py:177
  53.5 0.7 copy-done.7
  54.2 3.5 %collective-permute-start.5 = (f32[4,2,2,128,128]{4,3,2,1,0:T(8,128)}, f32[4,2,2,128,128]{4,3,2,1,0:T(8,128)}, u32[]{:S(2)}, u32[]{:S(2)}) collective-permute-start(f32[4,2,2,128,128]{4,3,2,1,0:T(8,128)} %get-tuple-element.24.refs_1_), channel_id=1, source_target_pairs={{0,31},{1,0},{2,1},{3,2},{4,3},{5,4},{6,5},{7,6},{8,7},{9,8},{10,9... | collective-permute-start | bytes 3145736 | tf_op jit(solution)/shard_map/ppermute | solution.py:581
  57.8 0.0 collective-permute-start.4
  57.8 7.9 %all-to-all-start.1 = ((f32[32,16,128]{2,1,0:T(8,128)}), f32[32,16,128]{2,1,0:T(8,128)S(1)}, u32[]{:S(2)}, u32[]{:S(2)}) async-start(f32[32,16,128]{2,1,0:T(8,128)} %bitcast.6), calls=%async_computation.1 | async-start | bytes 524288 | tf_op jit(solution)/shard_map/all_to_all | solution.py:682
  65.7 0.0 copy-start.8
  65.7 0.9 copy-done.8
  66.6 10.9 %sums.2.refs_0_ = f32[16,2,2,128,128]{4,3,2,1,0:T(8,128)S(1)} custom-call(f32[5,2,2,128,128]{4,3,2,1,0:T(8,128)} %get-tuple-element.23.refs_0_.last, f32[4,2,2,128,128]{4,3,2,1,0:T(8,128)} %get-tuple-element.24.refs_1_, f32[1,2,2,128,128]{4,3,2,1,0:T(8,128)S(1)} %get-tuple-element.25.refs_2_, f32[1,2,2,128,128]{4,3,2,1,0:T(8,128)S(1)} %copy-done.8, ...), custom_call_target="tpu_custom_call" | custom-call | flops 1000 | bytes 1000 | tf_op jit(solution)/shard_map/sums/pallas_call | solution.py:444
  77.6 1.4 %collective-permute-done.3.refs_2_.above = f32[5,2,2,128,128]{4,3,2,1,0:T(8,128)} collective-permute-done((f32[5,2,2,128,128]{4,3,2,1,0:T(8,128)}, f32[5,2,2,128,128]{4,3,2,1,0:T(8,128)}, u32[]{:S(2)}, u32[]{:S(2)}) %collective-permute-start.3) | collective-permute-done | bytes 1310752 | tf_op jit(solution)/shard_map/ppermute | solution.py:581
  79.0 2.9 %collective-permute-done.2.refs_1_.below = f32[5,2,2,128,128]{4,3,2,1,0:T(8,128)} collective-permute-done((f32[5,2,2,128,128]{4,3,2,1,0:T(8,128)}, f32[5,2,2,128,128]{4,3,2,1,0:T(8,128)}, u32[]{:S(2)}, u32[]{:S(2)}) %collective-permute-start.2) | collective-permute-done | bytes 1310752 | tf_op jit(solution)/shard_map/ppermute | solution.py:581
  81.9 0.0 copy-done.6
  81.9 4.5 %level.1 = f32[11,128,128]{2,1,0:T(8,128)S(1)} custom-call(f32[5,2,2,128,128]{4,3,2,1,0:T(8,128)} %collective-permute-done.2.refs_1_.below, f32[5,2,2,128,128]{4,3,2,1,0:T(8,128)} %get-tuple-element.28.refs_5_.own, f32[5,2,2,128,128]{4,3,2,1,0:T(8,128)} %get-tuple-element.23.refs_0_.last, f32[5,2,2,128,128]{4,3,2,1,0:T(8,128)} %collective-permute-done.3.refs_2_.above, ...), custom_call_target="tpu_custom_call" | custom-call | flops 1000 | bytes 1000 | tf_op jit(solution)/shard_map/level/pallas_call | solution.py:379
  86.4 0.0 copy-start.2
  86.4 0.9 copy-done.2
  87.3 3.5 %sums.3.acc = f32[16,2,2,128,128]{4,3,2,1,0:T(8,128)S(1)} custom-call(f32[16,2,2,128,128]{4,3,2,1,0:T(8,128)S(1)} %sums.2.refs_0_, f32[5,2,2,128,128]{4,3,2,1,0:T(8,128)} %collective-permute-done.2.refs_1_.below, f32[5,2,2,128,128]{4,3,2,1,0:T(8,128)} %collective-permute-done.3.refs_2_.above, f32[15,2,128,128]{3,2,1,0:T(8,128)S(1)} %bitcast.15), custom_call_target="tpu_custom_call" | custom-call | flops 1000 | bytes 1000 | tf_op jit(solution)/shard_map/sums/pallas_call | solution.py:444
  90.9 1.9 %copy-done = f32[16,2,2,128,128]{4,3,2,1,0:T(8,128)} copy-done((f32[16,2,2,128,128]{4,3,2,1,0:T(8,128)}, f32[16,2,2,128,128]{4,3,2,1,0:T(8,128)S(1)}, u32[]{:S(2)}) %copy-start) | copy-done | bytes 4194328
  92.8 13.9 %all-to-all-done.1.y_ref = f32[32,16,128]{2,1,0:T(8,128)S(1)} async-done(((f32[32,16,128]{2,1,0:T(8,128)}), f32[32,16,128]{2,1,0:T(8,128)S(1)}, u32[]{:S(2)}, u32[]{:S(2)}) %all-to-all-start.1) | async-done | bytes 262176 | tf_op jit(solution)/shard_map/all_to_all | solution.py:682
  106.8 0.0 collective-permute-done.5.far_high
  106.8 0.0 collective-permute-done.4.far_low
  106.8 12.2 %finish.1 = f32[4,16,128,128]{3,2,1,0:T(8,128)} custom-call(f32[16,2,2,128,128]{4,3,2,1,0:T(8,128)} %copy-done, f32[4,2,2,128,128]{4,3,2,1,0:T(8,128)} %collective-permute-done.4.far_low, f32[4,2,2,128,128]{4,3,2,1,0:T(8,128)} %collective-permute-done.5.far_high, f32[15,2,128,128]{3,2,1,0:T(8,128)S(1)} %bitcast.16, f32[11,128,128]{2,1,0:T(8,128)} %copy-done.2, ...), custom_call_target="tpu_custom_call" | custom-call | flops 1000 | bytes 1000 | tf_op jit(solution)/shard_map/finish/pallas_call | solution.py:533
  (16 shorter events, 0.0 us)
Async XLA Ops:
  0.0 0.9 copy-start.9
  1.0 0.8 copy-start.10
  1.8 25.7 %copy-start.15 = (f32[4,4,3,15]{3,1,2,0:T(4,128)S(1)}, f32[4,4,3,15]{3,1,2,0:T(4,128)}, u32[]{:S(2)}) copy-start(f32[4,4,3,15]{3,1,2,0:T(4,128)} %param.10) | copy-start | bytes 8644
  1.8 25.9 %copy-start.14 = (f32[15,1024]{1,0:T(8,128)S(1)}, f32[15,1024]{1,0:T(8,128)}, u32[]{:S(2)}) copy-start(f32[15,1024]{1,0:T(8,128)} %constant.21.clone) | copy-start | bytes 184324
  1.8 26.3 %copy-start.13 = (f32[1024,15]{1,0:T(8,128)S(1)}, f32[1024,15]{1,0:T(8,128)}, u32[]{:S(2)}) copy-start(f32[1024,15]{1,0:T(8,128)} %constant.22.clone) | copy-start | bytes 184324
  9.7 0.8 copy-start.3
  10.6 25.4 %all-to-all-start = ((f32[32,16,128]{2,1,0:T(8,128)}), f32[32,16,128]{2,1,0:T(8,128)S(1)}, u32[]{:S(2)}, u32[]{:S(2)}) async-start(f32[32,16,128]{2,1,0:T(8,128)} %get-tuple-element.21), calls=%async_computation | async-start | bytes 524288 | tf_op jit(solution)/shard_map/all_to_all | solution.py:673
  22.1 16.6 %collective-permute-start = (f32[2,128,128]{2,1,0:T(8,128)}, f32[2,128,128]{2,1,0:T(8,128)S(1)}, u32[]{:S(2)}, u32[]{:S(2)}) collective-permute-start(f32[2,128,128]{2,1,0:T(8,128)} %get-tuple-element.19), channel_id=1, source_target_pairs={{0,1},{1,2},{2,3},{3,4},{4,5},{5,6},{6,7},{7,8},{8,9},{9,10},{10,1... | collective-permute-start | bytes 393224 | tf_op jit(solution)/shard_map/ppermute | solution.py:581
  23.9 14.7 %collective-permute-start.1 = (f32[2,128,128]{2,1,0:T(8,128)}, f32[2,128,128]{2,1,0:T(8,128)S(1)}, u32[]{:S(2)}, u32[]{:S(2)}) collective-permute-start(f32[2,128,128]{2,1,0:T(8,128)} %get-tuple-element.20), channel_id=1, source_target_pairs={{0,31},{1,0},{2,1},{3,2},{4,3},{5,4},{6,5},{7,6},{8,7},{9,8},{10,9... | collective-permute-start | bytes 393224 | tf_op jit(solution)/shard_map/ppermute | solution.py:581
  31.5 1.1 copy-start.5
  32.5 0.6 copy-start.11
  35.9 0.8 copy-start.12
  36.7 1.9 %copy-start.1 = (bf16[8,256,256]{2,1,0:T(8,128)(2,1)S(1)}, bf16[8,256,256]{2,1,0:T(8,128)(2,1)}, u32[]{:S(2)}) copy-start(bf16[8,256,256]{2,1,0:T(8,128)(2,1)} %constant.18.clone.mats) | copy-start | bytes 3145732
  36.7 1.9 %copy-start.4 = (f32[9,128,128]{2,1,0:T(8,128)S(1)}, f32[9,128,128]{2,1,0:T(8,128)}, u32[]{:S(2)}) copy-start(f32[9,128,128]{2,1,0:T(8,128)} %copy-done.3) | copy-start | bytes 1769476
  44.5 34.5 %collective-permute-start.3 = (f32[5,2,2,128,128]{4,3,2,1,0:T(8,128)}, f32[5,2,2,128,128]{4,3,2,1,0:T(8,128)}, u32[]{:S(2)}, u32[]{:S(2)}) collective-permute-start(f32[5,2,2,128,128]{4,3,2,1,0:T(8,128)} %get-tuple-element.23.refs_0_.last), channel_id=1, source_target_pairs={{0,31},{1,0},{2,1},{3,2},{4,3},{5,4},{6,5},{7,6},{8,7},{9,8},{10,9... | collective-permute-start | bytes 3932168 | tf_op jit(solution)/shard_map/ppermute | solution.py:581
  44.5 37.4 %collective-permute-start.2 = (f32[5,2,2,128,128]{4,3,2,1,0:T(8,128)}, f32[5,2,2,128,128]{4,3,2,1,0:T(8,128)}, u32[]{:S(2)}, u32[]{:S(2)}) collective-permute-start(f32[5,2,2,128,128]{4,3,2,1,0:T(8,128)} %get-tuple-element.28.refs_5_.own), channel_id=1, source_target_pairs={{0,1},{1,2},{2,3},{3,4},{4,5},{5,6},{6,7},{7,8},{8,9},{9,10},{10,1... | collective-permute-start | bytes 3932168 | tf_op jit(solution)/shard_map/ppermute | solution.py:581
  53.5 0.7 copy-start.7
  54.2 52.5 %collective-permute-start.5 = (f32[4,2,2,128,128]{4,3,2,1,0:T(8,128)}, f32[4,2,2,128,128]{4,3,2,1,0:T(8,128)}, u32[]{:S(2)}, u32[]{:S(2)}) collective-permute-start(f32[4,2,2,128,128]{4,3,2,1,0:T(8,128)} %get-tuple-element.24.refs_1_), channel_id=1, source_target_pairs={{0,31},{1,0},{2,1},{3,2},{4,3},{5,4},{6,5},{7,6},{8,7},{9,8},{10,9... | collective-permute-start | bytes 3145736 | tf_op jit(solution)/shard_map/ppermute | solution.py:581
  57.8 49.0 %collective-permute-start.4 = (f32[4,2,2,128,128]{4,3,2,1,0:T(8,128)}, f32[4,2,2,128,128]{4,3,2,1,0:T(8,128)}, u32[]{:S(2)}, u32[]{:S(2)}) collective-permute-start(f32[4,2,2,128,128]{4,3,2,1,0:T(8,128)} %get-tuple-element.27.refs_4_), channel_id=1, source_target_pairs={{0,1},{1,2},{2,3},{3,4},{4,5},{5,6},{6,7},{7,8},{8,9},{9,10},{10,1... | collective-permute-start | bytes 3145736 | tf_op jit(solution)/shard_map/ppermute | solution.py:581
  57.8 49.0 %all-to-all-start.1 = ((f32[32,16,128]{2,1,0:T(8,128)}), f32[32,16,128]{2,1,0:T(8,128)S(1)}, u32[]{:S(2)}, u32[]{:S(2)}) async-start(f32[32,16,128]{2,1,0:T(8,128)} %bitcast.6), calls=%async_computation.1 | async-start | bytes 524288 | tf_op jit(solution)/shard_map/all_to_all | solution.py:682
  65.7 1.0 copy-start.8
  66.6 15.3 %copy-start.6 = (f32[15,128,128]{2,1,0:T(8,128)S(1)}, f32[15,128,128]{2,1,0:T(8,128)}, u32[]{:S(2)}) copy-start(f32[15,128,128]{2,1,0:T(8,128)} %copy-done.5) | copy-start | bytes 2949124
  86.4 0.9 copy-start.2
  90.9 2.0 %copy-start = (f32[16,2,2,128,128]{4,3,2,1,0:T(8,128)}, f32[16,2,2,128,128]{4,3,2,1,0:T(8,128)S(1)}, u32[]{:S(2)}) copy-start(f32[16,2,2,128,128]{4,3,2,1,0:T(8,128)S(1)} %sums.3.acc) | copy-start | bytes 12582916
